TPU v7x, 256 devices: a whole 4x4x8 slice. The times are simulated.
256 devices in a mesh: ia: 8 (over z_lo, core), wa: 4 (over y), ao: 8 (over z_hi, x).
Axes of the slice: x: 4, y: 4, z: 8 (z_hi: 2, z_lo: 4; z = z_hi * 4 + z_lo), core: 2. Of those that a mesh axis runs over, the one named last changes fastest.
Arguments:
- inputs: bfloat16 [1280, 12288], P('wa', ('ia', 'ao')), may hold values from -6 to 6
- out_grad: bfloat16 [1280, 12288], P('wa', ('ia', 'ao')), may hold values from -6 to 6
- preact: bfloat16 [1280, 24576], P('wa', 'ao'), may hold values from -6 to 6
- up_weight: bfloat16 [12288, 24576], P('ia', ('ao', 'wa')), may hold values from -0.0546875 to 0.0546875
- down_weight: bfloat16 [24576, 12288], P(('ao', 'wa'), 'ia'), may hold values from -0.0390625 to 0.0390625
Outputs:
- input_grad: bfloat16 [1280, 12288], P('wa', ('ia', 'ao'))
- up_grad: bfloat16 [12288, 24576], P('ia', ('ao', 'wa'))
- down_grad: bfloat16 [24576, 12288], P(('ao', 'wa'), 'ia')
All inputs are finite; a program needn't handle non-finite values.
Results may differ from a plain program's by a relative error of at most 0.025.
Values may be sent and summed in bfloat16 or wider, within the bound.
A program may use at most 128 MiB of HBM per device.

v0:
```python
import jax
import jax.numpy as jnp
from jax import lax
from jax.sharding import PartitionSpec as P


def gelu_parts(values):
    floats = values.astype(jnp.float32)
    square = floats * floats
    inner = 0.7978845608 * (floats + 0.044715 * floats * square)
    tangent = jnp.tanh(inner)
    activated = 0.5 * floats * (1.0 + tangent)
    derivative = 0.5 * (1.0 + tangent) + 0.5 * floats * (1.0 - tangent * tangent) * 0.7978845608 * (
        1.0 + 0.134145 * square
    )
    return (activated, derivative)


def per_device(inputs, out_grad, preact, up_weight, down_weight):
    up_tile, down_tile = (
        lax.all_gather(up_weight, "wa", axis=1, tiled=True),
        lax.all_gather(down_weight, "wa", axis=0, tiled=True),
    )
    in_rows, grad_rows = (
        lax.all_gather(inputs, "ao", axis=1, tiled=True),
        lax.all_gather(out_grad, "ao", axis=1, tiled=True),
    )
    activated, derivative = gelu_parts(preact)
    activated = activated.astype(jnp.bfloat16)
    partial_grad = jnp.einsum("td,fd->tf", grad_rows, down_tile, preferred_element_type=jnp.float32)
    act_grad = lax.psum(partial_grad.astype(jnp.bfloat16), "ia").astype(jnp.float32)
    hidden_grad = (act_grad * derivative).astype(jnp.bfloat16)
    down_grad = lax.psum_scatter(
        jnp.einsum("tf,td->fd", activated, grad_rows, preferred_element_type=jnp.float32).astype(
            jnp.bfloat16
        ),
        "wa",
        scatter_dimension=0,
        tiled=True,
    )
    up_term = jnp.einsum("td,tf->df", in_rows, hidden_grad, preferred_element_type=jnp.float32)
    up_grad = lax.psum_scatter(up_term.astype(jnp.bfloat16), "wa", scatter_dimension=1, tiled=True)
    input_term = jnp.einsum("tf,df->td", hidden_grad, up_tile, preferred_element_type=jnp.float32)
    input_grad = lax.psum_scatter(
        input_term.astype(jnp.bfloat16), "ao", scatter_dimension=1, tiled=True
    )
    return (input_grad, up_grad, down_grad)


def solution(mesh):
    placed = (
        P("wa", ("ia", "ao")),
        P("wa", ("ia", "ao")),
        P("wa", "ao"),
        P("ia", ("ao", "wa")),
        P(("ao", "wa"), "ia"),
    )
    return jax.shard_map(
        per_device,
        mesh=mesh,
        in_specs=placed,
        out_specs=(P("wa", ("ia", "ao")), P("ia", ("ao", "wa")), P(("ao", "wa"), "ia")),
        check_vma=False,
    )
```

profile of v0, /device:TPU:32, one launch (start us, length us, event | category | flops | bytes accessed | tf_op | source)
XLA Modules:
  0.0 590.4 jit_solution(16927216192474375937)
XLA Ops:
  7.2 0.0 all-gather.3.cloned.1.call-start
  7.2 0.7 all-gather.3.cloned.1.call-update
  7.9 0.0 all-reduce.2.cloned.1.call-start
  7.9 51.2 %all_gather.12 = bf16[320,1536]{0,1:T(8,128)(2,1)S(1)} all-gather(bf16[320,192]{0,1:T(8,128)(2,1)} %param.6), channel_id=1, replica_groups=mesh['ia'=8,'wa'=4,'ao'=8] {'ao'}, dimensions={1}, use_global_device_ids=true | all-gather | bytes 1105920 | tf_op jit(solution)/shard_map/all_gather | solution.py:26
  59.2 47.8 %all-gather.3.cloned.1.call-done = bf16[3072,1536]{1,0:T(8,128)(2,1)} async-done(((bf16[768,1536]{1,0:T(8,128)(2,1)}), bf16[3072,1536]{1,0:T(8,128)(2,1)}) %all-gather.3.cloned.1.call-update) | async-done | bytes 9437200 | tf_op jit(solution)/shard_map/all_gather | solution.py:22
  107.0 9.0 %convolution_convert_fusion.2 = bf16[320,3072]{1,0:T(8,128)(2,1)} fusion(bf16[320,1536]{0,1:T(8,128)(2,1)S(1)} %all_gather.12, bf16[3072,1536]{1,0:T(8,128)(2,1)} %all-gather.3.cloned.1.call-done), kind=kOutput, calls=%fused_computation.11 | convolution fusion | flops 3020881920 | bytes 12386304 | tf_op jit(solution)/shard_map/td,fd->tf/dot_general | solution.py:30
  116.0 0.0 all-reduce.2.cloned.1.call-update
  116.0 0.0 all-gather.5.cloned.1.call-start
  116.1 0.7 all-gather.5.cloned.1.call-update
  116.7 0.0 reduce-scatter.6.cloned.1.call-start
  116.8 0.1 copy-done
  116.9 55.9 %all_gather.15 = bf16[320,1536]{0,1:T(8,128)(2,1)S(1)} all-gather(bf16[320,192]{0,1:T(8,128)(2,1)S(1)} %copy-done), channel_id=1, replica_groups=mesh['ia'=8,'wa'=4,'ao'=8] {'ao'}, dimensions={1}, use_global_device_ids=true | all-gather | bytes 1105920 | tf_op jit(solution)/shard_map/all_gather | solution.py:25
  172.8 32.5 %all-reduce.2.cloned.1.call-done = bf16[320,3072]{1,0:T(8,128)(2,1)} async-done(((bf16[320,3072]{1,0:T(8,128)(2,1)}), bf16[320,3072]{1,0:T(8,128)(2,1)}) %all-reduce.2.cloned.1.call-update) | async-done | bytes 1966096 | tf_op jit(solution)/shard_map/psum | solution.py:31
  205.3 13.7 %fusion = bf16[1536,3072]{0,1:T(8,128)(2,1)} fusion(bf16[320,1536]{0,1:T(8,128)(2,1)S(1)} %all_gather.15, bf16[320,3072]{1,0:T(8,128)(2,1)} %param.7, bf16[320,3072]{1,0:T(8,128)(2,1)} %all-reduce.2.cloned.1.call-done), kind=kOutput, calls=%fused_computation.2 | convolution fusion | flops 3044278272 | bytes 14352384 | tf_op jit(solution)/shard_map/td,tf->df/dot_general | solution.py:41
  219.0 0.0 reduce-scatter.6.cloned.1.call-update
  219.0 0.2 reduce-scatter.4.cloned.1.call-start
  219.2 85.2 %all-gather.5.cloned.1.call-done = bf16[1536,3072]{1,0:T(8,128)(2,1)} async-done(((bf16[1536,768]{1,0:T(8,128)(2,1)}), bf16[1536,3072]{1,0:T(8,128)(2,1)}) %all-gather.5.cloned.1.call-update) | async-done | bytes 9437200 | tf_op jit(solution)/shard_map/all_gather | solution.py:21
  304.4 10.6 %convolution_convert_fusion.3 = bf16[320,1536]{0,1:T(8,128)(2,1)} fusion(bf16[1536,3072]{1,0:T(8,128)(2,1)} %all-gather.5.cloned.1.call-done, bf16[320,3072]{1,0:T(8,128)(2,1)S(1)} %copy-done.1, bf16[320,3072]{1,0:T(8,128)(2,1)} %all-reduce.2.cloned.1.call-done), kind=kOutput, calls=%fused_computation.21 | convolution fusion | flops 3040051200 | bytes 14352384 | tf_op jit(solution)/shard_map/tf,df->td/dot_general | solution.py:43
  315.1 0.0 reduce-scatter.8.cloned.1.call-start
  315.1 9.2 %convolution_convert_fusion = bf16[3072,1536]{1,0:T(8,128)(2,1)} fusion(bf16[320,1536]{0,1:T(8,128)(2,1)S(1)} %all_gather.12, bf16[320,3072]{1,0:T(8,128)(2,1)S(1)} %copy-done.1), kind=kOutput, calls=%fused_computation | convolution fusion | flops 3034447872 | bytes 12386304 | tf_op jit(solution)/shard_map/tf,td->fd/dot_general | solution.py:34
  324.3 75.3 %reduce-scatter.6.cloned.1.call-done = bf16[1536,768]{0,1:T(8,128)(2,1)} async-done(((bf16[1536,3072]{0,1:T(8,128)(2,1)}), bf16[1536,768]{0,1:T(8,128)(2,1)}) %reduce-scatter.6.cloned.1.call-update) | async-done | bytes 2359312 | tf_op jit(solution)/shard_map/reduce_scatter | solution.py:42
  399.7 4.3 copy.8
  403.9 87.1 %reduce-scatter.4.cloned.1.call-done = bf16[320,192]{0,1:T(8,128)(2,1)} async-done(((bf16[320,1536]{0,1:T(8,128)(2,1)}), bf16[320,192]{0,1:T(8,128)(2,1)}) %reduce-scatter.4.cloned.1.call-update) | async-done | bytes 122896 | tf_op jit(solution)/shard_map/reduce_scatter | solution.py:44
  491.0 92.5 %reduce-scatter.8.cloned.1.call-done = bf16[768,1536]{1,0:T(8,128)(2,1)} async-done(((bf16[3072,1536]{1,0:T(8,128)(2,1)}), bf16[768,1536]{1,0:T(8,128)(2,1)}) %reduce-scatter.8.cloned.1.call-update) | async-done | bytes 2359312 | tf_op jit(solution)/shard_map/reduce_scatter | solution.py:33
  (5 shorter events, 0.0 us)
Async XLA Ops:
  7.2 99.8 %all-gather.3.cloned.1.call-start = ((), (), s32[]{:S(2)}) async-start(), calls=%async_computation.3 | async-start | bytes 11796480 | tf_op jit(solution)/shard_map/all_gather | solution.py:22
  7.9 197.4 %all-reduce.2.cloned.1.call-start = ((), (), s32[]{:S(2)}) async-start(), calls=%async_computation.4 | async-start | bytes 3932160 | tf_op jit(solution)/shard_map/psum | solution.py:31
  116.0 0.9 copy-start
  116.0 188.4 %all-gather.5.cloned.1.call-start = ((), (), s32[]{:S(2)}) async-start(), calls=%async_computation.5 | async-start | bytes 11796480 | tf_op jit(solution)/shard_map/all_gather | solution.py:21
  116.7 282.9 %reduce-scatter.6.cloned.1.call-start = ((), (), s32[]{:S(2)}) async-start(), calls=%async_computation.7 | async-start | bytes 11796480 | tf_op jit(solution)/shard_map/reduce_scatter | solution.py:42
  219.0 85.5 %copy-start.1 = (bf16[320,3072]{1,0:T(8,128)(2,1)S(1)}, bf16[320,3072]{1,0:T(8,128)(2,1)}, u32[]{:S(2)}) copy-start(bf16[320,3072]{1,0:T(8,128)(2,1)} %param.7) | copy-start | bytes 5898244
  219.0 272.0 %reduce-scatter.4.cloned.1.call-start = ((), (), s32[]{:S(2)}) async-start(), calls=%async_computation.6 | async-start | bytes 1327104 | tf_op jit(solution)/shard_map/reduce_scatter | solution.py:44
  315.1 268.4 %reduce-scatter.8.cloned.1.call-start = ((), (), s32[]{:S(2)}) async-start(), calls=%async_computation.8 | async-start | bytes 11796480 | tf_op jit(solution)/shard_map/reduce_scatter | solution.py:33
Sparse Core Ops, SparseCore 0:
  9.8 97.1 all-gather.2
  116.1 89.1 all-reduce.1
  207.2 97.1 all-gather.4
  307.1 92.5 reduce-scatter.5
  404.6 86.3 reduce-scatter.3
  494.1 89.4 reduce-scatter.7
where the time goes:
time: 592 us; the launch traced here: 590 us
  waiting for transfers between devices  422 us (71%)
  blocking collectives  107 us (18%)
  matrix products  42.5 us (7%)
  between operations  14.1 us (2%)
    reduce_scatter x1, waiting for transfers between devices, per_device(): lax.psum_scatter(jnp.einsum('tf,td->fd', activated, grad_rows, preferred_...  92.5 us
    reduce_scatter x1, waiting for transfers between devices, per_device(): lax.psum_scatter(input_term.astype(jnp.bfloat16), 'ao', scatter_dimension...  87.1 us
    all_gather x1, waiting for transfers between devices, per_device(): lax.all_gather(up_weight, 'wa', axis=1, tiled=True)  85.2 us
    reduce_scatter x1, waiting for transfers between devices, per_device(): lax.psum_scatter(up_term.astype(jnp.bfloat16), 'wa', scatter_dimension=1,...  75.3 us
    all_gather x1, blocking collectives, per_device(): lax.all_gather(inputs, 'ao', axis=1, tiled=True)  55.9 us
    all_gather x1, blocking collectives, per_device(): lax.all_gather(out_grad, 'ao', axis=1, tiled=True)  51.2 us
    all_gather x1, waiting for transfers between devices, per_device(): lax.all_gather(down_weight, 'wa', axis=0, tiled=True)  47.8 us
    psum x1, waiting for transfers between devices, per_device(): lax.psum(partial_grad.astype(jnp.bfloat16), 'ia').astype(jnp.float32)  32.5 us
  transfers between devices with their start and end apart: 6, of which 6 were waited for; matrix products, arithmetic and copies ran while one was open for 6% of the time, Pallas kernels for 0%

commit v1 on v0

v1 whole, which is shorter than its diff:
```python
import jax
import jax.numpy as jnp
from jax import lax
from jax.sharding import PartitionSpec as P


def gelu_parts(values):
    floats = values.astype(jnp.float32)
    square = floats * floats
    inner = 0.7978845608 * (floats + 0.044715 * floats * square)
    tangent = jnp.tanh(inner)
    activated = 0.5 * floats * (1.0 + tangent)
    derivative = 0.5 * (1.0 + tangent) + 0.5 * floats * (1.0 - tangent * tangent) * 0.7978845608 * (
        1.0 + 0.134145 * square
    )
    return (activated, derivative)


def per_device(inputs, out_grad, preact, up_weight, down_weight):
    n_wa = lax.axis_size("wa")
    rows = inputs.shape[0]
    grad = lax.all_gather(out_grad, "ao", axis=1, tiled=True)
    grad = lax.all_gather(grad, "wa", axis=0, tiled=True)
    tokens = lax.all_gather(inputs, "ao", axis=1, tiled=True)
    tokens = lax.all_gather(tokens, "wa", axis=0, tiled=True)
    pre = lax.all_to_all(preact, "wa", split_axis=1, concat_axis=0, tiled=True)
    activated, derivative = gelu_parts(pre)
    activated = activated.astype(jnp.bfloat16)
    partial = jnp.einsum("td,fd->tf", grad, down_weight, preferred_element_type=jnp.float32)
    act_grad = lax.psum(partial.astype(jnp.bfloat16), "ia").astype(jnp.float32)
    hidden_grad = (act_grad * derivative).astype(jnp.bfloat16)
    down_grad = jnp.einsum(
        "tf,td->fd", activated, grad, preferred_element_type=jnp.float32
    ).astype(jnp.bfloat16)
    up_grad = jnp.einsum(
        "td,tf->df", tokens, hidden_grad, preferred_element_type=jnp.float32
    ).astype(jnp.bfloat16)
    term = jnp.einsum("tf,df->td", hidden_grad, up_weight, preferred_element_type=jnp.float32)
    term = lax.psum_scatter(term.astype(jnp.bfloat16), "wa", scatter_dimension=0, tiled=True)
    input_grad = lax.psum_scatter(term, "ao", scatter_dimension=1, tiled=True)
    return (input_grad, up_grad, down_grad)


def solution(mesh):
    placed = (
        P("wa", ("ia", "ao")),
        P("wa", ("ia", "ao")),
        P("wa", "ao"),
        P("ia", ("ao", "wa")),
        P(("ao", "wa"), "ia"),
    )
    return jax.shard_map(
        per_device,
        mesh=mesh,
        in_specs=placed,
        out_specs=(P("wa", ("ia", "ao")), P("ia", ("ao", "wa")), P(("ao", "wa"), "ia")),
        check_vma=False,
    )
```

time: 592 us -> 407 us (0.69)
  waiting for transfers between devices: 422 us -> 218 us
  blocking collectives: 107 us -> 128 us
  matrix products: 42.5 us -> 26.9 us
  local copies, waits for them, and re-layouts: 4.37 us -> 12.4 us
    reduce_scatter x3 -> x1, waiting for transfers between devices: 255 us -> 0.02 us  [per_device(): lax.psum_scatter(term.astype(jnp.bfloat16), 'wa', scatter_dimension=0, ti...]
    unnamed x6, waiting for transfers between devices: 1.43 us -> 72.9 us
    all_gather x2, waiting for transfers between devices: 133 us -> 97.8 us  [the longest x1 49.5 us: per_device(): grad = lax.all_gather(grad, 'wa', axis=0, tiled=True)]
    all_to_all x0 -> x1, blocking collectives: none -> 28.4 us  [per_device(): pre = lax.all_to_all(preact, 'wa', split_axis=1, concat_axis=0, tiled=True)]
    dot_general x4, matrix products: 42.5 us -> 26.9 us  [the longest x1 7.38 us: per_device(): jnp.einsum('td,fd->tf', grad, down_weight, preferred_element_type=jnp.flo...]
    psum x1, waiting for transfers between devices: 32.5 us -> 46.8 us  [per_device(): act_grad = lax.psum(partial.astype(jnp.bfloat16), 'ia').astype(jnp.float32)]
    all_gather x2, blocking collectives: 107 us -> 99.7 us  [the longest x1 51.3 us: per_device(): grad = lax.all_gather(out_grad, 'ao', axis=1, tiled=True)]
  transfers between devices with their start and end apart: 6 -> 5, of which waited for: 6 -> 4; matrix products, arithmetic and copies ran while one was open for 6% -> 6% of each run, Pallas kernels for 0% -> 0%
where the time goes in v1:
time: 407 us; the launch traced here: 405 us
  waiting for transfers between devices  218 us (54%)
  blocking collectives  128 us (31%)
  matrix products  26.9 us (7%)
  between operations  13.8 us (3%)
  local copies, waits for them, and re-layouts  12.4 us (3%)
  other arithmetic  5.36 us (1%)
    unnamed x6, waiting for transfers between devices  72.9 us
    all_gather x1, blocking collectives, per_device(): grad = lax.all_gather(out_grad, 'ao', axis=1, tiled=True)  51.3 us
    all_gather x1, waiting for transfers between devices, per_device(): grad = lax.all_gather(grad, 'wa', axis=0, tiled=True)  49.5 us
    all_gather x1, blocking collectives, per_device(): tokens = lax.all_gather(inputs, 'ao', axis=1, tiled=True)  48.4 us
    all_gather x1, waiting for transfers between devices, per_device(): tokens = lax.all_gather(tokens, 'wa', axis=0, tiled=True)  48.3 us
    psum x1, waiting for transfers between devices, per_device(): act_grad = lax.psum(partial.astype(jnp.bfloat16), 'ia').astype(jnp.float32)  46.8 us
    all_to_all x1, blocking collectives, per_device(): pre = lax.all_to_all(preact, 'wa', split_axis=1, concat_axis=0, tiled=True)  28.4 us
  transfers between devices with their start and end apart: 5, of which 4 were waited for; matrix products, arithmetic and copies ran while one was open for 6% of the time, Pallas kernels for 0%

profile of v1, /device:TPU:32, one launch (start us, length us, event | category | flops | bytes accessed | tf_op | source)
XLA Modules:
  0.0 404.6 jit_solution(58825703934003082)
XLA Ops:
  7.2 0.0 all-gather.3.cloned.1.call-start
  7.2 51.3 %all_gather.12 = bf16[320,1536]{0,1:T(8,128)(2,1)S(1)} all-gather(bf16[320,192]{0,1:T(8,128)(2,1)} %param.6), channel_id=1, replica_groups=mesh['ia'=8,'wa'=4,'ao'=8] {'ao'}, dimensions={1}, use_global_device_ids=true | all-gather | bytes 1105920 | tf_op jit(solution)/shard_map/all_gather | solution.py:22
  58.6 1.4 copy.16
  60.0 0.0 all-reduce.2.cloned.1.call-start
  60.0 49.5 %all-gather.3.cloned.1.call-done = bf16[1280,1536]{1,0:T(8,128)(2,1)} async-done(((bf16[320,1536]{1,0:T(8,128)(2,1)}), bf16[1280,1536]{1,0:T(8,128)(2,1)}) %all-gather.3.cloned.1.call-update) | async-done | bytes 3932176 | tf_op jit(solution)/shard_map/all_gather | solution.py:23
  109.5 7.4 %convolution_convert_fusion.3 = bf16[1280,768]{1,0:T(8,128)(2,1)} fusion(bf16[1280,1536]{1,0:T(8,128)(2,1)} %all-gather.3.cloned.1.call-done, bf16[768,1536]{1,0:T(8,128)(2,1)} %param.9), kind=kOutput, calls=%fused_computation.20 | convolution fusion | flops 3020881920 | bytes 8257536 | tf_op jit(solution)/shard_map/td,fd->tf/dot_general | solution.py:29
  116.9 0.0 reduce-scatter.5.cloned.1.call-start
  116.9 1.7 copy.25
  118.6 28.4 %all_to_all.13 = bf16[320,4,768]{2,0,1:T(8,128)(2,1)} all-to-all(bf16[320,4,768]{2,0,1:T(8,128)(2,1)S(1)} %bitcast.59), channel_id=1, replica_groups=mesh['ia'=8,'wa'=4,'ao'=8] {'wa'}, dimensions={1} | all-to-all | bytes 3932160 | tf_op jit(solution)/shard_map/all_to_all | solution.py:26
  147.0 46.8 %all-reduce.2.cloned.1.call-done = bf16[1280,768]{1,0:T(8,128)(2,1)} async-done(((bf16[1280,768]{1,0:T(8,128)(2,1)}), bf16[1280,768]{1,0:T(8,128)(2,1)}) %all-reduce.2.cloned.1.call-update) | async-done | bytes 1966096 | tf_op jit(solution)/shard_map/psum | solution.py:30
  193.8 5.4 %fusion.9 = (bf16[1280,768]{1,0:T(8,128)(2,1)}, bf16[1280,768]{1,0:T(8,128)(2,1)S(1)}) fusion(bf16[320,4,768]{2,0,1:T(8,128)(2,1)} %all_to_all.13, bf16[1280,768]{1,0:T(8,128)(2,1)} %all-reduce.2.cloned.1.call-done), kind=kLoop, calls=%fused_computation.14 | loop fusion | flops 21626880 | bytes 7864320 | tf_op jit(solution)/shard_map/convert_element_type | solution.py:28
  199.2 1.3 copy-done.1
  200.5 4.8 %convolution_convert_fusion = bf16[1280,1536]{1,0:T(8,128)(2,1)} fusion(bf16[1280,768]{1,0:T(8,128)(2,1)S(1)} %get-tuple-element.13, bf16[1536,768]{1,0:T(8,128)(2,1)S(1)} %copy-done), kind=kOutput, calls=%fused_computation | convolution fusion | flops 3021864960 | bytes 8257536 | tf_op jit(solution)/shard_map/tf,df->td/dot_general | solution.py:38
  205.3 0.0 all-gather.5.cloned.1.call-start
  205.4 48.4 %all_gather.14 = bf16[320,1536]{0,1:T(8,128)(2,1)S(1)} all-gather(bf16[320,192]{0,1:T(8,128)(2,1)} %param.5), channel_id=1, replica_groups=mesh['ia'=8,'wa'=4,'ao'=8] {'ao'}, dimensions={1}, use_global_device_ids=true | all-gather | bytes 1105920 | tf_op jit(solution)/shard_map/all_gather | solution.py:24
  253.8 1.4 copy.18
  255.2 0.2 reduce-scatter.7.cloned.1.call-start
  255.4 0.0 reduce-scatter.5.cloned.1.call-done
  255.4 2.4 copy.21
  257.9 48.3 %all-gather.5.cloned.1.call-done = bf16[1280,1536]{1,0:T(8,128)(2,1)} async-done(((bf16[320,1536]{1,0:T(8,128)(2,1)}), bf16[1280,1536]{1,0:T(8,128)(2,1)}) %all-gather.5.cloned.1.call-update) | async-done | bytes 3932176 | tf_op jit(solution)/shard_map/all_gather | solution.py:25
  306.2 7.4 %fusion.13 = bf16[1536,768]{0,1:T(8,128)(2,1)} fusion(bf16[1280,768]{1,0:T(8,128)(2,1)} %copy-done.1, bf16[1280,1536]{1,0:T(8,128)(2,1)} %all-gather.5.cloned.1.call-done), kind=kOutput, calls=%fused_computation.21 | convolution fusion | flops 3021078528 | bytes 8257536 | tf_op jit(solution)/shard_map/td,tf->df/dot_general | solution.py:35
  313.5 4.3 %copy.20 = bf16[1536,768]{1,0:T(8,128)(2,1)} copy(bf16[1536,768]{0,1:T(8,128)(2,1)} %fusion.13) | data formatting | bytes 4718592
  317.8 7.4 %convolution_convert_fusion.1 = bf16[768,1536]{1,0:T(8,128)(2,1)} fusion(bf16[1280,768]{1,0:T(8,128)(2,1)} %get-tuple-element.12, bf16[1280,1536]{1,0:T(8,128)(2,1)} %all-gather.3.cloned.1.call-done), kind=kOutput, calls=%fused_computation.18 | convolution fusion | flops 3021078528 | bytes 8257536 | tf_op jit(solution)/shard_map/tf,td->fd/dot_general | solution.py:32
  325.2 72.9 %reduce-scatter.7.cloned.1.call-done = bf16[192,320]{1,0:T(8,128)(2,1)} async-done(((bf16[1536,320]{1,0:T(8,128)(2,1)}), bf16[192,320]{1,0:T(8,128)(2,1)}) %reduce-scatter.7.cloned.1.call-update) | async-done | bytes 122896
  (8 shorter events, 0.1 us)
Async XLA Ops:
  7.2 193.3 %copy-start = (bf16[1536,768]{1,0:T(8,128)(2,1)S(1)}, bf16[1536,768]{1,0:T(8,128)(2,1)}, u32[]{:S(2)}) copy-start(bf16[1536,768]{1,0:T(8,128)(2,1)} %param.8) | copy-start | bytes 7077892
  7.2 102.3 %all-gather.3.cloned.1.call-start = ((), (), s32[]{:S(2)}) async-start(), calls=%async_computation.3 | async-start | bytes 4915200 | tf_op jit(solution)/shard_map/all_gather | solution.py:23
  60.0 133.9 %all-reduce.2.cloned.1.call-start = ((), (), s32[]{:S(2)}) async-start(), calls=%async_computation.4 | async-start | bytes 3932160 | tf_op jit(solution)/shard_map/psum | solution.py:30
  116.9 138.6 %reduce-scatter.5.cloned.1.call-start = ((), (), s32[]{:S(2)}) async-start(), calls=%async_computation.5 | async-start | bytes 4915200 | tf_op jit(solution)/shard_map/reduce_scatter | solution.py:39
  199.2 1.3 copy-start.1
  205.3 100.8 %all-gather.5.cloned.1.call-start = ((), (), s32[]{:S(2)}) async-start(), calls=%async_computation.6 | async-start | bytes 4915200 | tf_op jit(solution)/shard_map/all_gather | solution.py:25
  255.2 142.9 %reduce-scatter.7.cloned.1.call-start = ((), (), s32[]{:S(2)}) async-start(), calls=%async_computation.7 | async-start | bytes 1327104
Sparse Core Ops, SparseCore 0:
  60.1 49.3 all-gather.2
  117.0 76.8 all-reduce.1
  205.5 49.8 reduce-scatter.4
  257.7 48.3 all-gather.4
  311.1 86.8 reduce-scatter.6

commit v2 on v1

v2 whole, which is shorter than its diff:
```python
import jax
import jax.numpy as jnp
from jax import lax
from jax.experimental import pallas as pl
from jax.experimental.pallas import tpu as pltpu
from jax.sharding import PartitionSpec as P

MESH = pl.DeviceIdType.MESH
BF = jnp.bfloat16
F32 = jnp.float32
TOK = 320
FEAT = 192
BLK = 480
DI = 1536
HI = 768
NT = (((1,), (1,)), ((), ()))
TN = (((0,), (0,)), ((), ()))
FWD = (0, 3)


def gelu(u):
    square = u * u
    t = jnp.tanh(0.7978845608 * (u + 0.044715 * u * square))
    return 0.5 * u * (1.0 + t)


def slope(u):
    square = u * u
    t = jnp.tanh(0.7978845608 * (u + 0.044715 * u * square))
    return 0.5 * (1.0 + t) + 0.5 * u * (1.0 - t * t) * 0.7978845608 * (1.0 + 0.134145 * square)


def swap_halves(v):
    return pltpu.roll(v, 64, 1)


def low_lanes(shape):
    return lax.broadcasted_iota(jnp.int32, shape, 1) < 64


def loop(n, body):
    def step(i, carry):
        body(i)
        return carry

    lax.fori_loop(0, n, step, 0)


def kernel(
    grad_in, tok_in, preact, up_w, down_w,
    ig_out, ug_out, dg_out,
    cg, cx, ci, rs, g, xt, wd, wu, par, rc, r1, r2, s1, s2, pre, stage, act, hid, ug, dg,
    ag_send, ag_recv, rs_send, rs_recv, f_send, f_recv, p_send, p_recv, l_sem,
):
    ia, y, ao = lax.axis_index("ia"), lax.axis_index("wa"), lax.axis_index("ao")
    zl, c = ia // 2, ia % 2
    zh, x = ao // 4, ao % 4
    b0, b1 = zl % 2, zl // 2

    def dev(dx=0, dy=0, flip_zh=False, to_zl=None, flip_c=False):
        x_, y_ = (x + dx) % 4, (y + dy) % 4
        zh_ = 1 - zh if flip_zh else zh
        zl_ = zl if to_zl is None else to_zl
        c_ = 1 - c if flip_c else c
        return {"ia": zl_ * 2 + c_, "wa": y_, "ao": zh_ * 4 + x_}

    def dev_p(d):
        return dev(dx=d * (1 - c), dy=d * c)

    def dev_s(d):
        return dev(dx=d * c, dy=d * (1 - c))

    sibling = dev(flip_c=True)
    far_z = dev(flip_zh=True)
    zl1 = dev(to_zl=zl + 1 - 2 * b0)
    zl2 = dev(to_zl=zl + 2 - 4 * b1)

    sent = []

    def push(src, dst, ssem, rsem, to):
        copy = pltpu.make_async_remote_copy(
            src_ref=src, dst_ref=dst, send_sem=ssem, recv_sem=rsem, device_id=to, device_id_type=MESH
        )
        copy.start()
        sent.append(copy)

    def got(dst, rsem, frm):
        pltpu.make_async_remote_copy(
            src_ref=dst, dst_ref=dst, send_sem=l_sem.at[7], recv_sem=rsem, device_id=frm, device_id_type=MESH
        ).wait_recv()

    copies = [
        pltpu.make_async_copy(down_w, wd, l_sem.at[0]),
        pltpu.make_async_copy(up_w, wu, l_sem.at[1]),
        pltpu.make_async_copy(
            preact.at[:, pl.ds(pl.multiple_of(y * HI, 128), HI)], pre.at[0], l_sem.at[2]
        ),
    ]
    for copy in copies:
        copy.start()

    def slot(w, j, k, jr=None, kr=None):
        jr, kr = (j if jr is None else jr), (k if kr is None else kr)
        dx, dy = j + (k - j) * c, kr + (jr - kr) * c
        zh_ = 1 - zh if w else zh
        return dy * 8 + zh_ * 4 + (x + dx) % 4

    def pack(src, dst):
        own = slot(0, 0, 0)

        @pl.when(x % 2 == 0)
        def _():
            v = src[...].astype(F32)
            dst[own, 0:TOK, :] = v[:, 0:128].astype(BF)
            m = v[:, 128:192]
            dst[own, TOK:BLK, :] = jnp.concatenate([m[0:160], m[160:320]], axis=1).astype(BF)

        @pl.when(x % 2 == 1)
        def _():
            v = src[...].astype(F32)
            dst[own, 0:TOK, :] = v[:, 64:192].astype(BF)
            m = v[:, 0:64]
            dst[own, TOK:BLK, :] = jnp.concatenate([m[160:320], m[0:160]], axis=1).astype(BF)

    def unpack(src, dst, r):
        def body(n):
            e = src.at[r * 8 + 2 * n]
            o = src.at[r * 8 + 2 * n + 1]
            rows = pl.ds(r * TOK, TOK)
            base = n * 384
            dst[rows, pl.ds(pl.multiple_of(base, 128), 128)] = e[0:TOK, :]
            dst[rows, pl.ds(pl.multiple_of(base + 256, 128), 128)] = o[0:TOK, :]
            p, q = e[TOK:BLK, :].astype(F32), o[TOK:BLK, :].astype(F32)
            low = low_lanes((160, 128))
            mid = pl.ds(pl.multiple_of(base + 128, 128), 128)
            dst[pl.ds(r * TOK, 160), mid] = jnp.where(low, p, q).astype(BF)
            dst[pl.ds(r * TOK + 160, 160), mid] = swap_halves(jnp.where(low, q, p)).astype(BF)

        loop(4, body)

    pack(grad_in, cg)
    pack(tok_in, cx)

    barrier = pltpu.get_barrier_semaphore()
    partners = [dev_p(1), dev_p(3), dev_s(1), dev_s(3), dev(dy=2), sibling, far_z, zl1, zl2]
    for partner in partners[0:4] + partners[5:]:
        pl.semaphore_signal(barrier, inc=1, device_id=partner, device_id_type=MESH)
    pl.semaphore_wait(barrier, 8)

    class Gather:
        def __init__(self, index, buf):
            self.index, self.buf, self.n, self.have = index, buf, 0, {(0, 0, 0)}

        def _push(self, w, j, k, jr, kr, to, wr=None):
            push(
                self.buf.at[slot(w, j, k)],
                self.buf.at[slot(w, j, k, jr, kr)],
                ag_send.at[self.index, self.n],
                ag_recv.at[self.index, w if wr is None else wr, jr, kr],
                to,
            )
            self.n += 1

        def p(self, w, j, d):
            self._push(w, j, 0, (j - d) % 4, 0, dev_p(d))

        def s(self, w, j, k, d):
            self._push(w, j, k, j, (k - d) % 4, dev_s(d))

        def far(self):
            self._push(0, 0, 0, 0, 0, far_z, wr=1)

        def get(self, w, j, k):
            if (w, j, k) in self.have:
                return
            self.have.add((w, j, k))
            got(self.buf.at[slot(w, j, k)], ag_recv.at[self.index, w, j, k], dev_p(1))
            if k == 0:
                if j == 0:
                    self.start(w)
                    return
                if w == 0 and j == 3:
                    self.p(w, j, 1)
                if w == 1 and j == 1:
                    self.p(w, j, 3)
                self.s(w, j, k, 1)
                self.s(w, j, k, 3)
            elif k == 3 and j in FWD:
                self.s(w, j, k, 1)
            elif k == 1 and j not in FWD:
                self.s(w, j, k, 3)

        def start(self, w):
            for d in (1, 3):
                self.p(w, 0, d)
                self.s(w, 0, 0, d)

        def tokens(self, r):
            for w in (0, 1):
                for i in (0, 1, 3, 2):
                    self.get(w, i, r)
                for i in (0, 1, 3, 2):
                    self.get(w, r, i)

    grad, tok = Gather(0, cg), Gather(1, cx)

    half = pl.ds(pl.multiple_of(c * 160, 16), 160)
    other = pl.ds(pl.multiple_of((1 - c) * 160, 16), 160)
    up = 1 + 2 * c

    def preact_send():
        def cols(d):
            return pl.ds(pl.multiple_of(((y + d) % 4) * HI, 128), HI)

        push(preact.at[half, cols(2)], stage, p_send.at[0], p_recv.at[0], dev(dy=up))
        for d in (1, 3):
            push(preact.at[half, cols(d)], pre.at[4 - d, half], p_send.at[d], p_recv.at[4 - d], dev(dy=d))

    def preact_relay():
        got(stage, p_recv.at[0], dev(dy=1))
        push(stage, pre.at[2, half], p_send.at[2], p_recv.at[2], dev(dy=up))

    def preact_get(r):
        got(pre.at[r, half], p_recv.at[r], dev(dy=1))
        push(pre.at[r, half], pre.at[r, half], p_send.at[3 + r], p_recv.at[3 + r], sibling)

    def activate(r):
        if r > 0:
            got(pre.at[r, other], p_recv.at[3 + r], sibling)

        def body(i):
            rows = pl.multiple_of(i * 32, 32)
            u = pre[r, pl.ds(rows, 32), :].astype(F32)
            act[pl.ds(r * TOK + rows, 32), :] = gelu(u).astype(BF)

        loop(10, body)

    rows80 = pl.ds(pl.multiple_of(c * 160 + b0 * 80, 16), 80)
    keep80, give80 = pl.ds(pl.multiple_of(b0 * 80, 16), 80), pl.ds(pl.multiple_of((1 - b0) * 80, 16), 80)
    peer80 = pl.ds(pl.multiple_of(c * 160 + (1 - b0) * 80, 16), 80)
    keep384 = pl.ds(pl.multiple_of(b1 * 384, 128), 384)
    give384 = pl.ds(pl.multiple_of((1 - b1) * 384, 128), 384)

    def f1(r):
        grad.tokens(r)
        unpack(cg, g, r)
        if r == 0:
            copies[0].wait()

        def body(n):
            cols = pl.ds(pl.multiple_of(n * 256, 256), 256)
            par[r, :, cols] = lax.dot_general(
                g[r * TOK:(r + 1) * TOK, :], wd[cols, :], NT, preferred_element_type=F32
            ).astype(BF)

        loop(3, body)
        push(par.at[r, other], rc.at[r], f_send.at[0, r], f_recv.at[0, r], sibling)

    def f2(r):
        got(rc.at[r], f_recv.at[0, r], sibling)
        s1[r] = (par[r, half, :].astype(F32) + rc[r].astype(F32)).astype(BF)
        push(s1.at[r, give80], r1.at[r], f_send.at[1, r], f_recv.at[1, r], zl1)

    def f3(r):
        got(r1.at[r], f_recv.at[1, r], zl1)
        s2[r] = (s1[r, keep80, :].astype(F32) + r1[r].astype(F32)).astype(BF)
        push(s2.at[r, :, give384], r2.at[r], f_send.at[2, r], f_recv.at[2, r], zl2)

    def hrows(r, ds):
        return pl.ds(pl.multiple_of(r * TOK + ds.start, 16), ds.size)

    def f4(r):
        if r == 0:
            copies[2].wait()
        got(r2.at[r], f_recv.at[2, r], zl2)
        total = s2[r, :, keep384].astype(F32) + r2[r].astype(F32)
        u = pre[r, rows80, keep384].astype(F32)
        hid[hrows(r, rows80), keep384] = (total * slope(u)).astype(BF)
        piece = hid.at[hrows(r, rows80), keep384]
        push(piece, piece, f_send.at[3, r], f_recv.at[3, r], zl2)

    def f5(r):
        got(hid.at[hrows(r, rows80), give384], f_recv.at[3, r], zl2)
        piece = hid.at[hrows(r, rows80), :]
        push(piece, piece, f_send.at[4, r], f_recv.at[4, r], zl1)

    def f6(r):
        got(hid.at[hrows(r, peer80), :], f_recv.at[4, r], zl1)
        piece = hid.at[hrows(r, half), :]
        push(piece, piece, f_send.at[5, r], f_recv.at[5, r], sibling)

    def f7(r):
        got(hid.at[hrows(r, other), :], f_recv.at[5, r], sibling)
        if r == 0:
            copies[1].wait()

        def body(n):
            cols = pl.ds(pl.multiple_of(n * 384, 128), 384)
            term = lax.dot_general(
                hid[r * TOK:(r + 1) * TOK, :], wu[cols, :], NT, preferred_element_type=F32
            )
            even, odd = r * 8 + 2 * n, r * 8 + 2 * n + 1
            ci[even, 0:TOK, :] = term[:, 0:128].astype(BF)
            ci[odd, 0:TOK, :] = term[:, 256:384].astype(BF)
            top, bot = term[0:160, 128:256], swap_halves(term[160:320, 128:256])
            low = low_lanes((160, 128))
            ci[even, TOK:BLK, :] = jnp.where(low, top, bot).astype(BF)
            ci[odd, TOK:BLK, :] = jnp.where(low, bot, top).astype(BF)

        loop(4, body)

    def down(lo, hi):
        def body(i):
            cols = pl.ds(pl.multiple_of((lo + i) * 256, 256), 256)
            dg[:, cols] = lax.dot_general(act[...], g[:, cols], TN, preferred_element_type=F32).astype(BF)

        loop(hi - lo, body)

    def upg(lo, hi):
        def body(i):
            cols = pl.ds(pl.multiple_of((lo + i) * 256, 256), 256)
            ug[cols, :] = lax.dot_general(xt[:, cols], hid[...], TN, preferred_element_type=F32).astype(BF)

        loop(hi - lo, body)

    rs_count = []

    def rs_push(block, index, to):
        push(ci.at[block], rs.at[index], rs_send.at[index], rs_recv.at[index], to)

    def rs_add(block, *indices):
        total = ci[block].astype(F32)
        for index in indices:
            got(rs.at[index], rs_recv.at[index], dev_p(1))
            total = total + rs[index].astype(F32)
        return total

    def s_open(w, j):
        d, base = (1 if j in FWD else 3), (w * 4 + j) * 3
        rs_push(slot(w, j, 2), base, dev_s(d))
        rs_push(slot(w, j, 4 - d), base + 2, dev_s(4 - d))

    def s_mid(w, j):
        d, base = (1 if j in FWD else 3), (w * 4 + j) * 3
        block = slot(w, j, d)
        ci[block] = rs_add(block, base).astype(BF)
        rs_push(block, base + 1, dev_s(d))

    def s_end(w, j):
        base = (w * 4 + j) * 3
        block = slot(w, j, 0)
        ci[block] = rs_add(block, base + 1, base + 2).astype(BF)

    def p_open(w, j):
        d, base = (3 if w else 1), 24 + w * 3
        rs_push(slot(w, j, 0), base + (0 if j == 2 else 2), dev_p(d if j == 2 else 4 - d))

    def p_mid(w):
        d, base = (3 if w else 1), 24 + w * 3
        block = slot(w, d, 0)
        ci[block] = rs_add(block, base).astype(BF)
        rs_push(block, base + 1, dev_p(d))

    def p_end(w):
        base = 24 + w * 3
        block = slot(w, 0, 0)
        ci[block] = rs_add(block, base + 1, base + 2).astype(BF)
        if w:
            rs_push(block, 30, far_z)

    grad.far()
    grad.start(0)
    for key in ((0, 3, 0), (0, 1, 0), (0, 0, 3), (0, 0, 1), (0, 2, 0), (0, 1, 1), (0, 3, 3)):
        grad.get(*key)
    grad.get(1, 0, 0)
    tok.far()
    preact_send()
    for key in ((0, 2, 1), (0, 1, 3), (0, 3, 1), (0, 2, 3), (1, 3, 0), (1, 1, 0), (1, 0, 3), (1, 0, 1), (1, 2, 0)):
        grad.get(*key)
    f1(0)
    for key in ((1, 1, 1), (1, 3, 3), (1, 2, 1)):
        grad.get(*key)
    tok.start(0)
    f2(0)
    preact_relay()
    preact_get(1)
    preact_get(3)
    f1(1)
    f3(0)
    f1(3)
    f2(1)
    f4(0)
    tok.get(0, 3, 0)
    tok.get(0, 1, 0)
    f1(2)
    f2(3)
    f3(1)
    preact_get(2)
    f5(0)
    for key in ((0, 0, 3), (0, 0, 1), (1, 0, 0)):
        tok.get(*key)
    f2(2)
    f3(3)
    f4(1)
    f6(0)
    for key in ((0, 2, 0), (0, 1, 1), (0, 3, 3)):
        tok.get(*key)
    activate(0)
    f5(1)
    f3(2)
    f4(3)
    f7(0)
    for key in ((1, 3, 0), (1, 1, 0), (1, 0, 3), (1, 0, 1), (0, 2, 1)):
        tok.get(*key)
    f6(1)
    activate(1)
    f5(3)
    f4(2)
    f7(1)
    for key in ((1, 2, 0), (1, 1, 1), (1, 3, 3), (1, 2, 1)):
        tok.get(*key)
    activate(3)
    f6(3)
    f5(2)
    activate(2)
    f7(3)
    tok.tokens(0)
    f6(2)
    down(0, 3)
    f7(2)
    for j in (2, 1, 3, 0):
        s_open(1, j)
    down(3, 6)
    dg_copy = pltpu.make_async_copy(dg, dg_out, l_sem.at[3])
    dg_copy.start()
    for j in (2, 1, 3, 0):
        s_open(0, j)
    for j in (2, 1, 3, 0):
        s_mid(1, j)
    for r in (0, 1, 3, 2):
        tok.tokens(r)
    s_end(1, 2)
    p_open(1, 2)
    s_end(1, 1)
    p_open(1, 1)
    s_end(1, 3)
    p_mid(1)
    s_mid(0, 2)
    s_mid(0, 1)
    s_mid(0, 3)
    s_mid(0, 0)
    s_end(1, 0)
    p_end(1)
    for r in (0, 1, 2, 3):
        unpack(cx, xt, r)
    s_end(0, 2)
    p_open(0, 2)
    s_end(0, 3)
    p_open(0, 3)
    s_end(0, 1)
    upg(0, 2)
    p_mid(0)
    upg(2, 6)
    ug_copy = pltpu.make_async_copy(ug, ug_out, l_sem.at[4])
    ug_copy.start()
    s_end(0, 0)
    p_end(0)
    total = rs_add(slot(0, 0, 0), 30)
    mini = total[TOK:BLK, :]

    @pl.when(x % 2 == 0)
    def _():
        ig_out[:, 0:128] = total[0:TOK].astype(BF)
        ig_out[0:160, 128:192] = mini[:, 0:64].astype(BF)
        ig_out[160:320, 128:192] = mini[:, 64:128].astype(BF)

    @pl.when(x % 2 == 1)
    def _():
        ig_out[160:320, :] = jnp.concatenate([mini[:, 0:64], total[160:TOK]], axis=1).astype(BF)
        ig_out[0:160, :] = jnp.concatenate([mini[:, 64:128], total[0:160]], axis=1).astype(BF)

    dg_copy.wait()
    ug_copy.wait()
    for copy in sent:
        copy.wait_send()


def per_device(inputs, out_grad, preact, up_weight, down_weight):
    vmem = pl.BlockSpec(memory_space=pltpu.VMEM)
    hbm = pl.BlockSpec(memory_space=pl.ANY)
    blocks = pltpu.VMEM((32, BLK, 128), BF)
    dma = pltpu.SemaphoreType.DMA
    tokens = 4 * TOK
    return pl.pallas_call(
        kernel,
        out_shape=(
            jax.ShapeDtypeStruct((TOK, FEAT), BF),
            jax.ShapeDtypeStruct((DI, HI), BF),
            jax.ShapeDtypeStruct((HI, DI), BF),
        ),
        in_specs=[vmem, vmem, hbm, hbm, hbm],
        out_specs=(vmem, hbm, hbm),
        scratch_shapes=[
            blocks, blocks, blocks,
            pltpu.VMEM((31, BLK, 128), BF),
            pltpu.VMEM((tokens, DI), BF),
            pltpu.VMEM((tokens, DI), BF),
            pltpu.VMEM((HI, DI), BF),
            pltpu.VMEM((DI, HI), BF),
            pltpu.VMEM((4, TOK, HI), BF),
            pltpu.VMEM((4, 160, HI), BF),
            pltpu.VMEM((4, 80, HI), BF),
            pltpu.VMEM((4, 80, 384), BF),
            pltpu.VMEM((4, 160, HI), BF),
            pltpu.VMEM((4, 80, HI), BF),
            pltpu.VMEM((4, TOK, HI), BF),
            pltpu.VMEM((160, HI), BF),
            pltpu.VMEM((tokens, HI), BF),
            pltpu.VMEM((tokens, HI), BF),
            pltpu.VMEM((DI, HI), BF),
            pltpu.VMEM((HI, DI), BF),
            dma((2, 31)), dma((2, 2, 4, 4)),
            dma((31,)), dma((31,)),
            dma((6, 4)), dma((6, 4)),
            dma((7,)), dma((7,)),
            dma((8,)),
        ],
        compiler_params=pltpu.CompilerParams(
            collective_id=0, has_side_effects=True, vmem_limit_bytes=62 * 1024 * 1024
        ),
        name="ffn_backward",
    )(out_grad, inputs, preact, up_weight, down_weight)


def solution(mesh):
    placed = (
        P("wa", ("ia", "ao")),
        P("wa", ("ia", "ao")),
        P("wa", "ao"),
        P("ia", ("ao", "wa")),
        P(("ao", "wa"), "ia"),
    )
    return jax.shard_map(
        per_device,
        mesh=mesh,
        in_specs=placed,
        out_specs=(P("wa", ("ia", "ao")), P("ia", ("ao", "wa")), P(("ao", "wa"), "ia")),
        check_vma=False,
    )
```

time: 407 us -> 137 us (0.34)
  waiting for transfers between devices: 218 us -> 0 us
  blocking collectives: 128 us -> 0 us
  Pallas kernels: 0 us -> 126 us
  matrix products: 26.9 us -> 0 us
  between operations: 13.8 us -> 0.64 us
  other arithmetic: 5.36 us -> 0 us
    pallas_call x0 -> x1, Pallas kernels: none -> 126 us  [per_device(): pl.pallas_call(kernel, out_shape=(jax.ShapeDtypeStruct((TOK, FEAT), BF),...]
    all_gather x2 -> x0, blocking collectives: 99.7 us -> none  [the longest x1 51.3 us: per_device(): grad = lax.all_gather(out_grad, 'ao', axis=1, tiled=True)]
    all_gather x2 -> x0, waiting for transfers between devices: 97.8 us -> none  [the longest x1 49.5 us: per_device(): grad = lax.all_gather(grad, 'wa', axis=0, tiled=True)]
    unnamed x6 -> x0, waiting for transfers between devices: 72.9 us -> none
    psum x1 -> x0, waiting for transfers between devices: 46.8 us -> none  [per_device(): act_grad = lax.psum(partial.astype(jnp.bfloat16), 'ia').astype(jnp.float32)]
    all_to_all x1 -> x0, blocking collectives: 28.4 us -> none  [per_device(): pre = lax.all_to_all(preact, 'wa', split_axis=1, concat_axis=0, tiled=True)]
    dot_general x4 -> x0, matrix products: 26.9 us -> none  [the longest x1 7.38 us: per_device(): jnp.einsum('td,fd->tf', grad, down_weight, preferred_element_type=jnp.flo...]
    convert_element_type x1 -> x0, other arithmetic: 5.36 us -> none  [per_device(): activated = activated.astype(jnp.bfloat16)]
  transfers between devices with their start and end apart: 5 -> 0, of which waited for: 4 -> 0; matrix products, arithmetic and copies ran while one was open for 6% -> 0% of each run, Pallas kernels for 0% -> 0%
where the time goes in v2:
time: 137 us
  Pallas kernels  126 us (92%)
  local copies, waits for them, and re-layouts  9.87 us (7%)
    pallas_call x1, Pallas kernels, per_device(): pl.pallas_call(kernel, out_shape=(jax.ShapeDtypeStruct((TOK, FEAT), BF),...  126 us
    unnamed x6, local copies, waits for them, and re-layouts  8.17 us

profile of v2, /device:TPU:32, one launch (start us, length us, event | category | flops | bytes accessed | tf_op | source)
XLA Modules:
  0.0 136.8 jit_solution(17413411867951858861)
XLA Ops:
  0.6 1.7 %copy.9.tok_in = bf16[320,192]{1,0:T(8,128)(2,1)} copy(bf16[320,192]{0,1:T(8,128)(2,1)} %param.5) | data formatting | bytes 245760 | tf_op args[0]
  2.3 1.7 %copy.8.grad_in = bf16[320,192]{1,0:T(8,128)(2,1)} copy(bf16[320,192]{0,1:T(8,128)(2,1)} %param.6) | data formatting | bytes 245760 | tf_op args[1]
  4.0 126.3 %ffn_backward.1 = (bf16[320,192]{1,0:T(8,128)(2,1)}, bf16[1536,768]{1,0:T(8,128)(2,1)}, bf16[768,1536]{1,0:T(8,128)(2,1)}) custom-call(bf16[320,192]{1,0:T(8,128)(2,1)} %copy.8.grad_in, bf16[320,192]{1,0:T(8,128)(2,1)} %copy.9.tok_in, bf16[320,3072]{1,0:T(8,128)(2,1)} %preact.1, bf16[1536,768]{1,0:T(8,128)(2,1)} %up_w.1, bf16[768,1536]{1,0:T(8,128)(2,1)} %down_w.1), custom_call_target="tpu_custom_call" | custom-call | tf_op jit(solution)/shard_map/ffn_backward/pallas_call | solution.py:494
  130.3 1.7 %copy.10 = bf16[320,192]{0,1:T(8,128)(2,1)} copy(bf16[320,192]{1,0:T(8,128)(2,1)} %get-tuple-element.3) | data formatting | bytes 245760 | tf_op jit(solution)/shard_map/ffn_backward/pallas_call | solution.py:494
  132.0 0.0 copy-start
  132.0 3.4 %copy.13 = bf16[1536,768]{1,0:T(8,128)(2,1)} copy(bf16[1536,768]{1,0:T(8,128)(2,1)} %get-tuple-element.10) | data formatting | bytes 4718592
  135.4 0.0 copy-done
  135.4 1.4 %copy.14 = bf16[768,1536]{1,0:T(8,128)(2,1)} copy(bf16[768,1536]{1,0:T(8,128)(2,1)S(1)} %copy-done) | data formatting | bytes 4718592
Async XLA Ops:
  132.0 3.4 %copy-start = (bf16[768,1536]{1,0:T(8,128)(2,1)S(1)}, bf16[768,1536]{1,0:T(8,128)(2,1)}, u32[]{:S(2)}) copy-start(bf16[768,1536]{1,0:T(8,128)(2,1)} %get-tuple-element.11) | copy-start | bytes 7077892

commit v3 on v2

--- a/solution.py
+++ b/solution.py
@@ -48,8 +48,8 @@
 
 def kernel(
     grad_in, tok_in, preact, up_w, down_w,
-    ig_out, ug_out, dg_out,
-    cg, cx, ci, rs, g, xt, wd, wu, par, rc, r1, r2, s1, s2, pre, stage, act, hid, ug, dg,
+    ig_out, ug, dg,
+    cg, cx, ci, rs, g, xt, wd, wu, par, rc, r1, r2, s1, s2, pre, stage, act, hid,
     ag_send, ag_recv, rs_send, rs_recv, f_send, f_recv, p_send, p_recv, l_sem,
 ):
     ia, y, ao = lax.axis_index("ia"), lax.axis_index("wa"), lax.axis_index("ao")
@@ -108,19 +108,19 @@
     def pack(src, dst):
         own = slot(0, 0, 0)
 
+        def place(main, mini, first, second):
+            dst[own, 0:TOK, :] = src[main:main + 128, :].astype(F32).T.astype(BF)
+            m = src[mini:mini + 64, :].astype(F32).T
+            halves = (m[0:160], m[160:320])
+            dst[own, TOK:BLK, :] = jnp.concatenate([halves[first], halves[second]], axis=1).astype(BF)
+
         @pl.when(x % 2 == 0)
         def _():
-            v = src[...].astype(F32)
-            dst[own, 0:TOK, :] = v[:, 0:128].astype(BF)
-            m = v[:, 128:192]
-            dst[own, TOK:BLK, :] = jnp.concatenate([m[0:160], m[160:320]], axis=1).astype(BF)
+            place(0, 128, 0, 1)
 
         @pl.when(x % 2 == 1)
         def _():
-            v = src[...].astype(F32)
-            dst[own, 0:TOK, :] = v[:, 64:192].astype(BF)
-            m = v[:, 0:64]
-            dst[own, TOK:BLK, :] = jnp.concatenate([m[160:320], m[0:160]], axis=1).astype(BF)
+            place(64, 0, 1, 0)
 
     def unpack(src, dst, r):
         def body(n):
@@ -270,8 +270,6 @@
         return pl.ds(pl.multiple_of(r * TOK + ds.start, 16), ds.size)
 
     def f4(r):
-        if r == 0:
-            copies[2].wait()
         got(r2.at[r], f_recv.at[2, r], zl2)
         total = s2[r, :, keep384].astype(F32) + r2[r].astype(F32)
         u = pre[r, rows80, keep384].astype(F32)
@@ -323,10 +321,11 @@
 
         loop(hi - lo, body)
 
-    rs_count = []
-
     def rs_push(block, index, to):
-        push(ci.at[block], rs.at[index], rs_send.at[index], rs_recv.at[index], to)
+        pltpu.make_async_remote_copy(
+            src_ref=ci.at[block], dst_ref=rs.at[index], send_sem=rs_send.at[index], recv_sem=rs_recv.at[index],
+            device_id=to, device_id_type=MESH,
+        ).start()
 
     def rs_add(block, *indices):
         total = ci[block].astype(F32)
@@ -335,10 +334,12 @@
             total = total + rs[index].astype(F32)
         return total
 
-    def s_open(w, j):
-        d, base = (1 if j in FWD else 3), (w * 4 + j) * 3
-        rs_push(slot(w, j, 2), base, dev_s(d))
-        rs_push(slot(w, j, 4 - d), base + 2, dev_s(4 - d))
+    def s_far(w, j):
+        rs_push(slot(w, j, 2), (w * 4 + j) * 3, dev_s(1 if j in FWD else 3))
+
+    def s_near(w, j):
+        d = 3 if j in FWD else 1
+        rs_push(slot(w, j, d), (w * 4 + j) * 3 + 2, dev_s(d))
 
     def s_mid(w, j):
         d, base = (1 if j in FWD else 3), (w * 4 + j) * 3
@@ -368,138 +369,186 @@
         if w:
             rs_push(block, 30, far_z)
 
+    def early0(r):
+        for w in (1, 0):
+            for j in (2, 1, 3, 0):
+                if r == 2:
+                    s_far(w, j)
+                elif r == (3 if j in FWD else 1):
+                    s_near(w, j)
+                elif r:
+                    s_mid(w, j)
+
+    def early1(r):
+        last = {0: (), 2: (0,), 1: (2,), 3: (1,)}[r]
+        done = {0: (), 2: (), 1: (0,), 3: (2,)}[r]
+        for w in (1, 0):
+            for j in last:
+                s_mid(w, j)
+            s_far(w, r)
+            s_near(w, r)
+        for w in (1, 0):
+            for j in done:
+                s_end(w, j)
+                if j == 2:
+                    p_open(w, 2)
+
+    def tail0(part):
+        if part < 2:
+            w = 1 - part
+            near, far = (1, 3) if w else (3, 1)
+            s_end(w, 2)
+            p_open(w, 2)
+            s_end(w, near)
+            p_open(w, near)
+            s_end(w, far)
+            p_mid(w)
+        else:
+            s_end(3 - part, 0)
+            p_end(3 - part)
+
+    def tail1(part):
+        if part == 0:
+            s_mid(1, 3)
+            s_mid(0, 3)
+            s_end(1, 1)
+            p_open(1, 1)
+        elif part == 1:
+            s_end(0, 1)
+            p_mid(0)
+            s_end(1, 3)
+            p_mid(1)
+        elif part == 2:
+            s_end(0, 3)
+            p_open(0, 3)
+            p_end(1)
+        else:
+            p_end(0)
+
+    def by_core(first, second, *args):
+        @pl.when(c == 0)
+        def _():
+            first(*args)
+
+        @pl.when(c == 1)
+        def _():
+            second(*args)
+
+    def early(r):
+        by_core(early0, early1, r)
+
+    def gets(gather, *keys):
+        for key in keys:
+            gather.get(*key)
+
     grad.far()
     grad.start(0)
-    for key in ((0, 3, 0), (0, 1, 0), (0, 0, 3), (0, 0, 1), (0, 2, 0), (0, 1, 1), (0, 3, 3)):
-        grad.get(*key)
-    grad.get(1, 0, 0)
+    gets(grad, (0, 3, 0), (0, 1, 0), (0, 0, 3), (0, 0, 1), (1, 0, 0))
+    gets(grad, (0, 2, 0), (0, 1, 1), (0, 3, 3))
     tok.far()
+    gets(grad, (0, 2, 1), (1, 3, 0), (1, 1, 0), (1, 0, 3), (1, 0, 1))
     preact_send()
-    for key in ((0, 2, 1), (0, 1, 3), (0, 3, 1), (0, 2, 3), (1, 3, 0), (1, 1, 0), (1, 0, 3), (1, 0, 1), (1, 2, 0)):
-        grad.get(*key)
+    gets(grad, (1, 2, 0), (1, 1, 1), (1, 3, 3))
     f1(0)
-    for key in ((1, 1, 1), (1, 3, 3), (1, 2, 1)):
-        grad.get(*key)
+    gets(grad, (1, 2, 1))
     tok.start(0)
+    copies[2].wait()
+    activate(0)
     f2(0)
     preact_relay()
+    f3(0)
+    f1(2)
     preact_get(1)
     preact_get(3)
+    f4(0)
+    f2(2)
+    gets(tok, (0, 3, 0), (0, 1, 0), (0, 0, 3), (0, 0, 1), (1, 0, 0))
     f1(1)
-    f3(0)
+    f5(0)
+    f3(2)
+    f2(1)
     f1(3)
-    f2(1)
-    f4(0)
-    tok.get(0, 3, 0)
-    tok.get(0, 1, 0)
-    f1(2)
+    preact_get(2)
+    f6(0)
+    f4(2)
+    gets(tok, (0, 2, 0), (0, 1, 1), (0, 3, 3))
+    f3(1)
     f2(3)
-    f3(1)
-    preact_get(2)
-    f5(0)
-    for key in ((0, 0, 3), (0, 0, 1), (1, 0, 0)):
-        tok.get(*key)
-    f2(2)
+    f7(0)
+    early(0)
+    f5(2)
+    gets(tok, (0, 2, 1), (1, 3, 0), (1, 1, 0), (1, 0, 3), (1, 0, 1))
+    activate(1)
+    f4(1)
     f3(3)
-    f4(1)
-    f6(0)
-    for key in ((0, 2, 0), (0, 1, 1), (0, 3, 3)):
-        tok.get(*key)
-    activate(0)
+    f6(2)
+    activate(3)
+    f7(2)
+    early(2)
     f5(1)
-    f3(2)
     f4(3)
-    f7(0)
-    for key in ((1, 3, 0), (1, 1, 0), (1, 0, 3), (1, 0, 1), (0, 2, 1)):
-        tok.get(*key)
+    gets(tok, (1, 2, 0), (1, 1, 1), (1, 3, 3), (1, 2, 1))
+    activate(2)
+    down(0, 2)
     f6(1)
-    activate(1)
     f5(3)
-    f4(2)
     f7(1)
-    for key in ((1, 2, 0), (1, 1, 1), (1, 3, 3), (1, 2, 1)):
-        tok.get(*key)
-    activate(3)
+    early(1)
+    down(2, 4)
     f6(3)
-    f5(2)
-    activate(2)
+    for r in (0, 1):
+        tok.tokens(r)
+        unpack(cx, xt, r)
     f7(3)
-    tok.tokens(0)
-    f6(2)
-    down(0, 3)
-    f7(2)
-    for j in (2, 1, 3, 0):
-        s_open(1, j)
-    down(3, 6)
-    dg_copy = pltpu.make_async_copy(dg, dg_out, l_sem.at[3])
-    dg_copy.start()
-    for j in (2, 1, 3, 0):
-        s_open(0, j)
-    for j in (2, 1, 3, 0):
-        s_mid(1, j)
-    for r in (0, 1, 3, 2):
+    early(3)
+    for r in (3, 2):
         tok.tokens(r)
-    s_end(1, 2)
-    p_open(1, 2)
-    s_end(1, 1)
-    p_open(1, 1)
-    s_end(1, 3)
-    p_mid(1)
-    s_mid(0, 2)
-    s_mid(0, 1)
-    s_mid(0, 3)
-    s_mid(0, 0)
-    s_end(1, 0)
-    p_end(1)
-    for r in (0, 1, 2, 3):
         unpack(cx, xt, r)
-    s_end(0, 2)
-    p_open(0, 2)
-    s_end(0, 3)
-    p_open(0, 3)
-    s_end(0, 1)
-    upg(0, 2)
-    p_mid(0)
-    upg(2, 6)
-    ug_copy = pltpu.make_async_copy(ug, ug_out, l_sem.at[4])
-    ug_copy.start()
-    s_end(0, 0)
-    p_end(0)
+    by_core(tail0, tail1, 0)
+    upg(0, 1)
+    by_core(tail0, tail1, 1)
+    upg(1, 3)
+    by_core(tail0, tail1, 2)
+    upg(3, 6)
+    down(4, 6)
+    by_core(tail0, tail1, 3)
     total = rs_add(slot(0, 0, 0), 30)
-    mini = total[TOK:BLK, :]
+    main, left, right = total[0:TOK], total[TOK:BLK, 0:64], total[TOK:BLK, 64:128]
 
     @pl.when(x % 2 == 0)
     def _():
-        ig_out[:, 0:128] = total[0:TOK].astype(BF)
-        ig_out[0:160, 128:192] = mini[:, 0:64].astype(BF)
-        ig_out[160:320, 128:192] = mini[:, 64:128].astype(BF)
+        ig_out[0:128, :] = main.T.astype(BF)
+        ig_out[128:192, :] = jnp.concatenate([left, right], axis=0).T.astype(BF)
 
     @pl.when(x % 2 == 1)
     def _():
-        ig_out[160:320, :] = jnp.concatenate([mini[:, 0:64], total[160:TOK]], axis=1).astype(BF)
-        ig_out[0:160, :] = jnp.concatenate([mini[:, 64:128], total[0:160]], axis=1).astype(BF)
-
-    dg_copy.wait()
-    ug_copy.wait()
+        ig_out[64:192, :] = main.T.astype(BF)
+        ig_out[0:64, :] = jnp.concatenate([right, left], axis=0).T.astype(BF)
+
     for copy in sent:
         copy.wait_send()
+    for index in range(31):
+        pltpu.make_async_remote_copy(
+            src_ref=ci.at[0], dst_ref=rs.at[index], send_sem=rs_send.at[index], recv_sem=rs_recv.at[index],
+            device_id=far_z, device_id_type=MESH,
+        ).wait_send()
 
 
 def per_device(inputs, out_grad, preact, up_weight, down_weight):
     vmem = pl.BlockSpec(memory_space=pltpu.VMEM)
-    hbm = pl.BlockSpec(memory_space=pl.ANY)
+    hbm = pl.BlockSpec(memory_space=pltpu.HBM)
     blocks = pltpu.VMEM((32, BLK, 128), BF)
     dma = pltpu.SemaphoreType.DMA
     tokens = 4 * TOK
-    return pl.pallas_call(
+    input_grad, up_grad, down_grad = pl.pallas_call(
         kernel,
         out_shape=(
-            jax.ShapeDtypeStruct((TOK, FEAT), BF),
-            jax.ShapeDtypeStruct((DI, HI), BF),
-            jax.ShapeDtypeStruct((HI, DI), BF),
+            jax.ShapeDtypeStruct((FEAT, TOK), BF),
+            pltpu.VMEM((DI, HI), BF),
+            pltpu.VMEM((HI, DI), BF),
         ),
         in_specs=[vmem, vmem, hbm, hbm, hbm],
-        out_specs=(vmem, hbm, hbm),
+        out_specs=(vmem, vmem, vmem),
         scratch_shapes=[
             blocks, blocks, blocks,
             pltpu.VMEM((31, BLK, 128), BF),
@@ -517,8 +566,6 @@
             pltpu.VMEM((160, HI), BF),
             pltpu.VMEM((tokens, HI), BF),
             pltpu.VMEM((tokens, HI), BF),
-            pltpu.VMEM((DI, HI), BF),
-            pltpu.VMEM((HI, DI), BF),
             dma((2, 31)), dma((2, 2, 4, 4)),
             dma((31,)), dma((31,)),
             dma((6, 4)), dma((6, 4)),
@@ -526,10 +573,11 @@
             dma((8,)),
         ],
         compiler_params=pltpu.CompilerParams(
-            collective_id=0, has_side_effects=True, vmem_limit_bytes=62 * 1024 * 1024
+            collective_id=0, has_side_effects=True, vmem_limit_bytes=54 * 1024 * 1024
         ),
         name="ffn_backward",
-    )(out_grad, inputs, preact, up_weight, down_weight)
+    )(out_grad.T, inputs.T, preact, up_weight, down_weight)
+    return input_grad.T, up_grad, down_grad
 
 
 def solution(mesh):

time: 137 us -> 126 us (0.920); the launches traced: 137 us -> 124 us
  local copies, waits for them, and re-layouts: 9.87 us -> 3.48 us
  Pallas kernels: 126 us -> 120 us
    pallas_call x1, Pallas kernels: 126 us -> 120 us  [per_device(): pl.pallas_call(kernel, out_shape=(jax.ShapeDtypeStruct((FEAT, TOK), BF),...]
    unnamed x6 -> x5, local copies, waits for them, and re-layouts: 8.17 us -> 3.48 us
    pallas_call x1 -> x0, local copies, waits for them, and re-layouts: 1.7 us -> none  [per_device(): pl.pallas_call(kernel, out_shape=(jax.ShapeDtypeStruct((TOK, FEAT), BF),...]
where the time goes in v3:
time: 126 us; the launch traced here: 124 us
  Pallas kernels  120 us (95%)
  local copies, waits for them, and re-layouts  3.48 us (3%)
    pallas_call x1, Pallas kernels, per_device(): pl.pallas_call(kernel, out_shape=(jax.ShapeDtypeStruct((FEAT, TOK), BF),...  120 us
    unnamed x5, local copies, waits for them, and re-layouts  3.48 us

profile of v3, /device:TPU:32, one launch (start us, length us, event | category | flops | bytes accessed | tf_op | source)
XLA Modules:
  0.0 124.0 jit_solution(7471200869182513844)
XLA Ops:
  0.6 119.9 %ffn_backward.1 = (bf16[192,320]{1,0:T(8,128)(2,1)}, bf16[1536,768]{1,0:T(8,128)(2,1)S(1)}, bf16[768,1536]{1,0:T(8,128)(2,1)S(1)}) custom-call(bf16[192,320]{1,0:T(8,128)(2,1)} %bitcast.3, bf16[192,320]{1,0:T(8,128)(2,1)} %bitcast.4, bf16[320,3072]{1,0:T(8,128)(2,1)} %preact.1, bf16[1536,768]{1,0:T(8,128)(2,1)} %up_w.1, bf16[768,1536]{1,0:T(8,128)(2,1)} %down_w.1), custom_call_target="tpu_custom_call" | custom-call | tf_op jit(solution)/shard_map/ffn_backward/pallas_call | solution.py:543
  120.5 1.4 %copy.11 = bf16[1536,768]{1,0:T(8,128)(2,1)} copy(bf16[1536,768]{1,0:T(8,128)(2,1)S(1)} %get-tuple-element.10) | data formatting | bytes 4718592
  121.9 0.0 copy-start
  121.9 1.4 %copy.12 = bf16[768,1536]{1,0:T(8,128)(2,1)} copy(bf16[768,1536]{1,0:T(8,128)(2,1)S(1)} %get-tuple-element.11) | data formatting | bytes 4718592
  123.3 0.0 copy-done
  123.3 0.7 copy.13
Async XLA Ops:
  121.9 1.4 %copy-start = (bf16[192,320]{1,0:T(8,128)(2,1)S(1)}, bf16[192,320]{1,0:T(8,128)(2,1)}, u32[]{:S(2)}) copy-start(bf16[192,320]{1,0:T(8,128)(2,1)} %get-tuple-element.6) | copy-start | bytes 368644

commit v4 on v3

--- a/solution.py
+++ b/solution.py
@@ -17,6 +17,122 @@
 TN = (((0,), (0,)), ((), ()))
 FWD = (0, 3)
 
+ORDER = (
+    ("grad", 0, 0, 0), ("grad",), ("grad", 0, 3, 0), ("tok",), ("activate", 0), ("grad", 0, 1, 0),
+    ("grad", 1, 0, 0), ("grad", 0, 0, 3), ("grad", 0, 1, 1), ("grad", 1, 0, 3), ("grad", 1, 1, 0),
+    ("grad", 1, 3, 0), ("grad", 0, 0, 1), ("grad", 0, 3, 3), ("grad", 0, 1, 3), ("grad", 0, 2, 0),
+    ("grad", 1, 2, 0), ("grad", 1, 0, 1), ("grad", 1, 1, 1), ("grad", 0, 0, 2), ("grad", 1, 0, 2), ("f1", 0),
+    ("grad", 1, 3, 3), ("tok", 1, 0, 0), ("grad", 1, 3, 1), ("grad", 0, 3, 2), ("grad", 0, 2, 3),
+    ("grad", 0, 2, 1), ("f2", 0), ("grad", 1, 2, 1), ("grad", 0, 1, 2), ("grad", 0, 3, 1), ("grad", 1, 1, 3),
+    ("grad", 1, 1, 2), ("f1", 1), ("grad", 1, 3, 2), ("grad", 1, 2, 3), ("pre_send",), ("f1", 3), ("f3", 0),
+    ("f2", 1), ("grad", 1, 2, 2), ("grad", 0, 2, 2), ("tok", 1, 0, 1), ("tok", 1, 1, 0), ("f1", 2), ("f2", 3),
+    ("f2", 2), ("f3", 1), ("f4", 0), ("tok", 0, 0, 0), ("pre_relay",), ("f3", 2), ("pre_get", 1),
+    ("tok", 1, 0, 3), ("tok", 1, 3, 0), ("f4", 1), ("tok", 1, 2, 0), ("pre_get", 3), ("tok", 0, 3, 0),
+    ("tok", 0, 0, 1), ("f5", 0), ("tok", 0, 1, 0), ("pre_get", 2), ("tok", 1, 1, 1), ("f4", 2), ("f5", 1),
+    ("f6", 0), ("f3", 3), ("tok", 0, 0, 3), ("tok", 1, 1, 3), ("activate", 2), ("tok", 1, 3, 3), ("activate", 1),
+    ("f5", 2), ("tok", 0, 2, 0), ("f6", 1), ("activate", 3), ("tok", 0, 1, 1), ("tok", 1, 2, 1), ("tok", 0, 3, 3),
+    ("f4", 3), ("f7", 0), ("tok", 0, 2, 1),
+    ("scatter",
+     (),
+     (("near", 1, 0), ("far", 0, 0),)),
+    ("f6", 2), ("f7", 1), ("tok", 0, 3, 1),
+    ("scatter",
+     (),
+     (("far", 1, 1), ("near", 1, 1),)),
+    ("f5", 3), ("tok", 1, 2, 2), ("tok", 1, 0, 2), ("f7", 2),
+    ("scatter",
+     (),
+     (("far", 0, 2),)),
+    ("tok", 1, 1, 2),
+    ("scatter",
+     (),
+     (("far", 1, 2),)),
+    ("tok", 0, 2, 2),
+    ("scatter",
+     (("far", 0, 1),),
+     (("near", 0, 2),)),
+    ("down", 0, 1),
+    ("scatter",
+     (("far", 1, 3),),
+     ()),
+    ("tok", 0, 1, 3),
+    ("scatter",
+     (("far", 1, 2),),
+     ()),
+    ("tok", 1, 3, 2),
+    ("scatter",
+     (("far", 1, 1),),
+     ()),
+    ("tok", 1, 2, 3),
+    ("scatter",
+     (),
+     (("near", 0, 1),)),
+    ("f6", 3),
+    ("scatter",
+     (("near", 1, 2), ("far", 0, 0),),
+     ()),
+    ("down", 1, 2),
+    ("scatter",
+     (("near", 1, 1), ("far", 1, 0),),
+     (("mid", 1, 1),)),
+    ("tok", 0, 1, 2),
+    ("scatter",
+     (("far", 0, 2),),
+     (("near", 1, 2), ("far", 0, 1),)),
+    ("f7", 3),
+    ("scatter",
+     (("mid", 1, 2),),
+     (("far", 1, 3), ("mid", 1, 2),)),
+    ("tok", 0, 3, 2), ("down", 2, 3),
+    ("scatter",
+     (("mid", 1, 1), ("mid", 1, 3), ("near", 0, 2), ("mid", 0, 2),),
+     (("near", 1, 3), ("far", 1, 0),)),
+    ("down", 3, 4),
+    ("scatter",
+     (("near", 1, 3),),
+     (("mid", 0, 2), ("mid", 1, 3), ("near", 0, 3), ("end", 1, 2), ("p_open", 1, 2), ("far", 0, 3),)),
+    ("tok", 0, 2, 3),
+    ("scatter",
+     (),
+     (("mid", 1, 0),)),
+    ("tok", 1, 3, 1), ("down", 4, 5),
+    ("scatter",
+     (("near", 1, 0), ("far", 0, 3), ("mid", 1, 0),),
+     ()),
+    ("tok", 0, 0, 2),
+    ("scatter",
+     (("end", 1, 2), ("p_open", 1, 2),),
+     (("end", 1, 1),)),
+    ("unpack", 0), ("unpack", 1),
+    ("scatter",
+     (("end", 1, 1), ("mid", 0, 0),),
+     (("end", 0, 2), ("mid", 0, 1), ("p_open", 1, 1), ("near", 0, 0), ("mid", 0, 0), ("p_open", 0, 2), ("end", 1, 3), ("p_mid", 1), ("mid", 0, 3),)),
+    ("unpack", 3),
+    ("scatter",
+     (("p_open", 1, 1), ("near", 0, 0),),
+     ()),
+    ("unpack", 2),
+    ("scatter",
+     (("mid", 0, 1), ("end", 1, 3), ("end", 0, 2), ("near", 0, 1),),
+     ()),
+    ("upg", 0, 1),
+    ("scatter",
+     (("p_open", 0, 2), ("near", 0, 3), ("p_mid", 1),),
+     ()),
+    ("upg", 1, 3),
+    ("scatter",
+     (("mid", 0, 3), ("end", 1, 0), ("p_end", 1), ("end", 0, 1), ("end", 0, 3), ("p_mid", 0), ("p_open", 0, 3),),
+     (("end", 1, 0), ("p_end", 1), ("end", 0, 1), ("p_mid", 0), ("end", 0, 3),)),
+    ("upg", 3, 4), ("down", 5, 6),
+    ("scatter",
+     (("end", 0, 0),),
+     (("p_open", 0, 3), ("end", 0, 0),)),
+    ("upg", 4, 6),
+    ("scatter",
+     (("p_end", 0),),
+     (("p_end", 0),)),
+)
+
 
 def gelu(u):
     square = u * u
@@ -98,6 +214,12 @@
     ]
     for copy in copies:
         copy.start()
+    waiting = {0, 1, 2}
+
+    def loaded(n):
+        if n in waiting:
+            waiting.remove(n)
+            copies[n].wait()
 
     def slot(w, j, k, jr=None, kr=None):
         jr, kr = (j if jr is None else jr), (k if kr is None else kr)
@@ -227,6 +349,8 @@
     def activate(r):
         if r > 0:
             got(pre.at[r, other], p_recv.at[3 + r], sibling)
+        else:
+            loaded(2)
 
         def body(i):
             rows = pl.multiple_of(i * 32, 32)
@@ -244,8 +368,7 @@
     def f1(r):
         grad.tokens(r)
         unpack(cg, g, r)
-        if r == 0:
-            copies[0].wait()
+        loaded(0)
 
         def body(n):
             cols = pl.ds(pl.multiple_of(n * 256, 256), 256)
@@ -270,6 +393,8 @@
         return pl.ds(pl.multiple_of(r * TOK + ds.start, 16), ds.size)
 
     def f4(r):
+        if r == 0:
+            loaded(2)
         got(r2.at[r], f_recv.at[2, r], zl2)
         total = s2[r, :, keep384].astype(F32) + r2[r].astype(F32)
         u = pre[r, rows80, keep384].astype(F32)
@@ -289,8 +414,7 @@
 
     def f7(r):
         got(hid.at[hrows(r, other), :], f_recv.at[5, r], sibling)
-        if r == 0:
-            copies[1].wait()
+        loaded(1)
 
         def body(n):
             cols = pl.ds(pl.multiple_of(n * 384, 128), 384)
@@ -369,149 +493,42 @@
         if w:
             rs_push(block, 30, far_z)
 
-    def early0(r):
-        for w in (1, 0):
-            for j in (2, 1, 3, 0):
-                if r == 2:
-                    s_far(w, j)
-                elif r == (3 if j in FWD else 1):
-                    s_near(w, j)
-                elif r:
-                    s_mid(w, j)
-
-    def early1(r):
-        last = {0: (), 2: (0,), 1: (2,), 3: (1,)}[r]
-        done = {0: (), 2: (), 1: (0,), 3: (2,)}[r]
-        for w in (1, 0):
-            for j in last:
-                s_mid(w, j)
-            s_far(w, r)
-            s_near(w, r)
-        for w in (1, 0):
-            for j in done:
-                s_end(w, j)
-                if j == 2:
-                    p_open(w, 2)
-
-    def tail0(part):
-        if part < 2:
-            w = 1 - part
-            near, far = (1, 3) if w else (3, 1)
-            s_end(w, 2)
-            p_open(w, 2)
-            s_end(w, near)
-            p_open(w, near)
-            s_end(w, far)
-            p_mid(w)
+    gathers = {"grad": grad, "tok": tok}
+    steps = {
+        "pre_send": preact_send, "pre_relay": preact_relay, "pre_get": preact_get, "activate": activate,
+        "f1": f1, "f2": f2, "f3": f3, "f4": f4, "f5": f5, "f6": f6, "f7": f7,
+        "unpack": lambda r: unpack(cx, xt, r), "down": down, "upg": upg,
+    }
+    scatter = {
+        "far": s_far, "near": s_near, "mid": s_mid, "end": s_end,
+        "p_open": p_open, "p_mid": p_mid, "p_end": p_end,
+    }
+
+    def run(name, *args):
+        if name in gathers:
+            gather = gathers[name]
+            if args == (0, 0, 0):
+                gather.start(0)
+            elif args:
+                gather.get(*args)
+            else:
+                gather.far()
         else:
-            s_end(3 - part, 0)
-            p_end(3 - part)
-
-    def tail1(part):
-        if part == 0:
-            s_mid(1, 3)
-            s_mid(0, 3)
-            s_end(1, 1)
-            p_open(1, 1)
-        elif part == 1:
-            s_end(0, 1)
-            p_mid(0)
-            s_end(1, 3)
-            p_mid(1)
-        elif part == 2:
-            s_end(0, 3)
-            p_open(0, 3)
-            p_end(1)
+            steps[name](*args)
+
+    def by_core(core, work):
+        if work:
+            @pl.when(c == core)
+            def _():
+                for name, *args in work:
+                    scatter[name](*args)
+
+    for item in ORDER:
+        if item[0] == "scatter":
+            by_core(0, item[1])
+            by_core(1, item[2])
         else:
-            p_end(0)
-
-    def by_core(first, second, *args):
-        @pl.when(c == 0)
-        def _():
-            first(*args)
-
-        @pl.when(c == 1)
-        def _():
-            second(*args)
-
-    def early(r):
-        by_core(early0, early1, r)
-
-    def gets(gather, *keys):
-        for key in keys:
-            gather.get(*key)
-
-    grad.far()
-    grad.start(0)
-    gets(grad, (0, 3, 0), (0, 1, 0), (0, 0, 3), (0, 0, 1), (1, 0, 0))
-    gets(grad, (0, 2, 0), (0, 1, 1), (0, 3, 3))
-    tok.far()
-    gets(grad, (0, 2, 1), (1, 3, 0), (1, 1, 0), (1, 0, 3), (1, 0, 1))
-    preact_send()
-    gets(grad, (1, 2, 0), (1, 1, 1), (1, 3, 3))
-    f1(0)
-    gets(grad, (1, 2, 1))
-    tok.start(0)
-    copies[2].wait()
-    activate(0)
-    f2(0)
-    preact_relay()
-    f3(0)
-    f1(2)
-    preact_get(1)
-    preact_get(3)
-    f4(0)
-    f2(2)
-    gets(tok, (0, 3, 0), (0, 1, 0), (0, 0, 3), (0, 0, 1), (1, 0, 0))
-    f1(1)
-    f5(0)
-    f3(2)
-    f2(1)
-    f1(3)
-    preact_get(2)
-    f6(0)
-    f4(2)
-    gets(tok, (0, 2, 0), (0, 1, 1), (0, 3, 3))
-    f3(1)
-    f2(3)
-    f7(0)
-    early(0)
-    f5(2)
-    gets(tok, (0, 2, 1), (1, 3, 0), (1, 1, 0), (1, 0, 3), (1, 0, 1))
-    activate(1)
-    f4(1)
-    f3(3)
-    f6(2)
-    activate(3)
-    f7(2)
-    early(2)
-    f5(1)
-    f4(3)
-    gets(tok, (1, 2, 0), (1, 1, 1), (1, 3, 3), (1, 2, 1))
-    activate(2)
-    down(0, 2)
-    f6(1)
-    f5(3)
-    f7(1)
-    early(1)
-    down(2, 4)
-    f6(3)
-    for r in (0, 1):
-        tok.tokens(r)
-        unpack(cx, xt, r)
-    f7(3)
-    early(3)
-    for r in (3, 2):
-        tok.tokens(r)
-        unpack(cx, xt, r)
-    by_core(tail0, tail1, 0)
-    upg(0, 1)
-    by_core(tail0, tail1, 1)
-    upg(1, 3)
-    by_core(tail0, tail1, 2)
-    upg(3, 6)
-    down(4, 6)
-    by_core(tail0, tail1, 3)
+            run(*item)
     total = rs_add(slot(0, 0, 0), 30)
     main, left, right = total[0:TOK], total[TOK:BLK, 0:64], total[TOK:BLK, 64:128]
 

time: 126 us -> 116 us (0.921); the launches traced: 124 us -> 115 us
  Pallas kernels: 120 us -> 111 us
    pallas_call x1, Pallas kernels: 120 us -> 111 us  [per_device(): pl.pallas_call(kernel, out_shape=(jax.ShapeDtypeStruct((FEAT, TOK), BF),...]
where the time goes in v4:
time: 116 us; the launch traced here: 115 us
  Pallas kernels  111 us (96%)
  local copies, waits for them, and re-layouts  3.48 us (3%)
    pallas_call x1, Pallas kernels, per_device(): pl.pallas_call(kernel, out_shape=(jax.ShapeDtypeStruct((FEAT, TOK), BF),...  111 us
    unnamed x5, local copies, waits for them, and re-layouts  3.48 us

profile of v4, /device:TPU:32, one launch (start us, length us, event | category | flops | bytes accessed | tf_op | source)
XLA Modules:
  0.0 115.5 jit_solution(13695006081236170150)
XLA Ops:
  0.6 111.3 %ffn_backward.1 = (bf16[192,320]{1,0:T(8,128)(2,1)}, bf16[1536,768]{1,0:T(8,128)(2,1)S(1)}, bf16[768,1536]{1,0:T(8,128)(2,1)S(1)}) custom-call(bf16[192,320]{1,0:T(8,128)(2,1)} %bitcast.3, bf16[192,320]{1,0:T(8,128)(2,1)} %bitcast.4, bf16[320,3072]{1,0:T(8,128)(2,1)} %preact.1, bf16[1536,768]{1,0:T(8,128)(2,1)} %up_w.1, bf16[768,1536]{1,0:T(8,128)(2,1)} %down_w.1), custom_call_target="tpu_custom_call" | custom-call | tf_op jit(solution)/shard_map/ffn_backward/pallas_call | solution.py:560
  112.0 1.4 %copy.11 = bf16[1536,768]{1,0:T(8,128)(2,1)} copy(bf16[1536,768]{1,0:T(8,128)(2,1)S(1)} %get-tuple-element.10) | data formatting | bytes 4718592
  113.4 0.0 copy-start
  113.4 1.4 %copy.12 = bf16[768,1536]{1,0:T(8,128)(2,1)} copy(bf16[768,1536]{1,0:T(8,128)(2,1)S(1)} %get-tuple-element.11) | data formatting | bytes 4718592
  114.8 0.0 copy-done
  114.8 0.7 copy.13
Async XLA Ops:
  113.4 1.4 %copy-start = (bf16[192,320]{1,0:T(8,128)(2,1)S(1)}, bf16[192,320]{1,0:T(8,128)(2,1)}, u32[]{:S(2)}) copy-start(bf16[192,320]{1,0:T(8,128)(2,1)} %get-tuple-element.6) | copy-start | bytes 368644

commit v5 on v4

--- a/solution.py
+++ b/solution.py
@@ -18,116 +18,119 @@
 FWD = (0, 3)
 
 ORDER = (
-    ("grad", 0, 0, 0), ("grad",), ("grad", 0, 3, 0), ("tok",), ("activate", 0), ("grad", 0, 1, 0),
-    ("grad", 1, 0, 0), ("grad", 0, 0, 3), ("grad", 0, 1, 1), ("grad", 1, 0, 3), ("grad", 1, 1, 0),
-    ("grad", 1, 3, 0), ("grad", 0, 0, 1), ("grad", 0, 3, 3), ("grad", 0, 1, 3), ("grad", 0, 2, 0),
-    ("grad", 1, 2, 0), ("grad", 1, 0, 1), ("grad", 1, 1, 1), ("grad", 0, 0, 2), ("grad", 1, 0, 2), ("f1", 0),
-    ("grad", 1, 3, 3), ("tok", 1, 0, 0), ("grad", 1, 3, 1), ("grad", 0, 3, 2), ("grad", 0, 2, 3),
-    ("grad", 0, 2, 1), ("f2", 0), ("grad", 1, 2, 1), ("grad", 0, 1, 2), ("grad", 0, 3, 1), ("grad", 1, 1, 3),
-    ("grad", 1, 1, 2), ("f1", 1), ("grad", 1, 3, 2), ("grad", 1, 2, 3), ("pre_send",), ("f1", 3), ("f3", 0),
-    ("f2", 1), ("grad", 1, 2, 2), ("grad", 0, 2, 2), ("tok", 1, 0, 1), ("tok", 1, 1, 0), ("f1", 2), ("f2", 3),
-    ("f2", 2), ("f3", 1), ("f4", 0), ("tok", 0, 0, 0), ("pre_relay",), ("f3", 2), ("pre_get", 1),
-    ("tok", 1, 0, 3), ("tok", 1, 3, 0), ("f4", 1), ("tok", 1, 2, 0), ("pre_get", 3), ("tok", 0, 3, 0),
-    ("tok", 0, 0, 1), ("f5", 0), ("tok", 0, 1, 0), ("pre_get", 2), ("tok", 1, 1, 1), ("f4", 2), ("f5", 1),
-    ("f6", 0), ("f3", 3), ("tok", 0, 0, 3), ("tok", 1, 1, 3), ("activate", 2), ("tok", 1, 3, 3), ("activate", 1),
-    ("f5", 2), ("tok", 0, 2, 0), ("f6", 1), ("activate", 3), ("tok", 0, 1, 1), ("tok", 1, 2, 1), ("tok", 0, 3, 3),
-    ("f4", 3), ("f7", 0), ("tok", 0, 2, 1),
+    ("grad", 0, 0, 0), ("grad",), ("grad", 0, 3, 0), ("grad", 0, 1, 0), ("grad", 1, 0, 0), ("tok",),
+    ("grad", 0, 0, 3), ("grad", 0, 2, 0), ("grad", 1, 0, 3), ("grad", 1, 1, 0), ("grad", 1, 3, 0),
+    ("grad", 0, 0, 2), ("grad", 0, 1, 1), ("activate", 0), ("grad", 0, 3, 1), ("grad", 0, 0, 1),
+    ("grad", 1, 0, 1), ("grad", 0, 3, 3), ("grad", 1, 0, 2), ("grad", 1, 2, 0), ("grad", 1, 1, 1), ("f1", 0),
+    ("grad", 1, 3, 3), ("grad", 0, 1, 2), ("grad", 0, 2, 1), ("grad", 1, 2, 1), ("pre_send",), ("grad", 1, 1, 3),
+    ("f2", 0), ("grad", 0, 1, 3), ("grad", 1, 1, 2), ("grad", 1, 3, 1), ("f1", 1), ("grad", 0, 2, 2),
+    ("grad", 0, 2, 3), ("grad", 0, 3, 2), ("tok", 1, 0, 0), ("grad", 1, 3, 2), ("grad", 1, 2, 3), ("f3", 0),
+    ("f2", 1), ("grad", 1, 2, 2), ("f1", 2), ("pre_relay",), ("f4", 0), ("tok", 0, 0, 0), ("f2", 2), ("f3", 1),
+    ("pre_get", 1), ("tok", 1, 1, 0), ("f5", 0), ("f1", 3), ("f3", 2), ("tok", 0, 3, 0), ("f4", 1),
+    ("tok", 0, 1, 0), ("pre_get", 2), ("tok", 0, 0, 1), ("tok", 0, 0, 3), ("f2", 3), ("activate", 1), ("f6", 0),
+    ("f4", 2), ("tok", 1, 2, 0), ("tok", 0, 2, 0), ("f5", 1), ("tok", 0, 3, 3), ("tok", 0, 1, 3),
+    ("tok", 1, 3, 0), ("tok", 0, 1, 1), ("f3", 3), ("f7", 0), ("tok", 1, 0, 3), ("f5", 2), ("f6", 1),
+    ("pre_get", 3), ("tok", 0, 2, 1), ("tok", 1, 2, 1),
     ("scatter",
      (),
      (("near", 1, 0), ("far", 0, 0),)),
-    ("f6", 2), ("f7", 1), ("tok", 0, 3, 1),
-    ("scatter",
-     (),
-     (("far", 1, 1), ("near", 1, 1),)),
-    ("f5", 3), ("tok", 1, 2, 2), ("tok", 1, 0, 2), ("f7", 2),
-    ("scatter",
-     (),
-     (("far", 0, 2),)),
-    ("tok", 1, 1, 2),
-    ("scatter",
-     (),
-     (("far", 1, 2),)),
-    ("tok", 0, 2, 2),
-    ("scatter",
-     (("far", 0, 1),),
-     (("near", 0, 2),)),
-    ("down", 0, 1),
-    ("scatter",
-     (("far", 1, 3),),
+    ("f4", 3), ("tok", 0, 2, 3), ("tok", 1, 3, 3), ("f7", 1), ("f6", 2),
+    ("scatter",
+     (("near", 1, 2),),
+     (("far", 1, 0), ("far", 0, 1), ("far", 1, 1),)),
+    ("tok", 1, 2, 3),
+    ("scatter",
+     (),
+     (("near", 0, 1),)),
+    ("f5", 3), ("tok", 1, 1, 1), ("tok", 0, 3, 2),
+    ("scatter",
+     (("near", 0, 2),),
      ()),
-    ("tok", 0, 1, 3),
+    ("tok", 1, 0, 2), ("activate", 3), ("f7", 2),
+    ("scatter",
+     (("far", 1, 3), ("far", 1, 1),),
+     (("mid", 1, 0),)),
+    ("f6", 3),
+    ("scatter",
+     (),
+     (("near", 1, 1),)),
+    ("activate", 2),
     ("scatter",
      (("far", 1, 2),),
      ()),
+    ("tok", 0, 3, 1),
+    ("scatter",
+     (("far", 1, 0), ("far", 0, 0), ("far", 0, 1), ("far", 0, 3), ("near", 1, 1),),
+     (("far", 1, 2),)),
+    ("tok", 1, 3, 1), ("tok", 0, 0, 2),
+    ("scatter",
+     (("far", 0, 2),),
+     (("mid", 1, 1), ("mid", 0, 0),)),
+    ("tok", 1, 1, 2), ("f7", 3),
+    ("scatter",
+     (("mid", 1, 2),),
+     (("far", 1, 3), ("near", 1, 3), ("near", 1, 2), ("mid", 1, 2),)),
+    ("down", 0, 1),
+    ("scatter",
+     (("mid", 1, 1), ("near", 0, 3),),
+     (("far", 0, 3), ("end", 1, 0),)),
+    ("down", 1, 2),
+    ("scatter",
+     (("mid", 1, 3), ("mid", 0, 0),),
+     (("far", 0, 2), ("end", 1, 1),)),
+    ("tok", 1, 1, 3),
+    ("scatter",
+     (("near", 1, 3),),
+     ()),
+    ("down", 2, 3),
+    ("scatter",
+     (("end", 1, 2), ("p_open", 1, 2), ("mid", 0, 2),),
+     (("mid", 1, 3),)),
+    ("down", 3, 4),
+    ("scatter",
+     (),
+     (("end", 1, 2),)),
     ("tok", 1, 3, 2),
     ("scatter",
-     (("far", 1, 1),),
-     ()),
-    ("tok", 1, 2, 3),
-    ("scatter",
-     (),
-     (("near", 0, 1),)),
-    ("f6", 3),
-    ("scatter",
-     (("near", 1, 2), ("far", 0, 0),),
-     ()),
-    ("down", 1, 2),
-    ("scatter",
-     (("near", 1, 1), ("far", 1, 0),),
-     (("mid", 1, 1),)),
+     (("mid", 1, 0), ("end", 1, 1), ("p_open", 1, 1), ("near", 1, 0),),
+     (("p_open", 1, 2),)),
+    ("down", 4, 5), ("tok", 1, 0, 1),
+    ("scatter",
+     (("mid", 0, 3), ("end", 1, 3), ("p_mid", 1), ("near", 0, 0),),
+     (("near", 0, 2), ("mid", 0, 2),)),
+    ("unpack", 0),
+    ("scatter",
+     (),
+     (("p_open", 1, 1),)),
     ("tok", 0, 1, 2),
     ("scatter",
-     (("far", 0, 2),),
-     (("near", 1, 2), ("far", 0, 1),)),
-    ("f7", 3),
-    ("scatter",
-     (("mid", 1, 2),),
-     (("far", 1, 3), ("mid", 1, 2),)),
-    ("tok", 0, 3, 2), ("down", 2, 3),
-    ("scatter",
-     (("mid", 1, 1), ("mid", 1, 3), ("near", 0, 2), ("mid", 0, 2),),
-     (("near", 1, 3), ("far", 1, 0),)),
-    ("down", 3, 4),
-    ("scatter",
-     (("near", 1, 3),),
-     (("mid", 0, 2), ("mid", 1, 3), ("near", 0, 3), ("end", 1, 2), ("p_open", 1, 2), ("far", 0, 3),)),
-    ("tok", 0, 2, 3),
-    ("scatter",
-     (),
-     (("mid", 1, 0),)),
-    ("tok", 1, 3, 1), ("down", 4, 5),
-    ("scatter",
-     (("near", 1, 0), ("far", 0, 3), ("mid", 1, 0),),
-     ()),
-    ("tok", 0, 0, 2),
-    ("scatter",
-     (("end", 1, 2), ("p_open", 1, 2),),
-     (("end", 1, 1),)),
-    ("unpack", 0), ("unpack", 1),
-    ("scatter",
-     (("end", 1, 1), ("mid", 0, 0),),
-     (("end", 0, 2), ("mid", 0, 1), ("p_open", 1, 1), ("near", 0, 0), ("mid", 0, 0), ("p_open", 0, 2), ("end", 1, 3), ("p_mid", 1), ("mid", 0, 3),)),
+     (),
+     (("mid", 0, 3),)),
     ("unpack", 3),
     ("scatter",
-     (("p_open", 1, 1), ("near", 0, 0),),
+     (),
+     (("end", 1, 3), ("mid", 0, 1), ("p_mid", 1),)),
+    ("tok", 1, 2, 2), ("tok", 0, 2, 2),
+    ("scatter",
+     (("end", 0, 2),),
      ()),
     ("unpack", 2),
     ("scatter",
-     (("mid", 0, 1), ("end", 1, 3), ("end", 0, 2), ("near", 0, 1),),
-     ()),
-    ("upg", 0, 1),
-    ("scatter",
-     (("p_open", 0, 2), ("near", 0, 3), ("p_mid", 1),),
-     ()),
-    ("upg", 1, 3),
-    ("scatter",
-     (("mid", 0, 3), ("end", 1, 0), ("p_end", 1), ("end", 0, 1), ("end", 0, 3), ("p_mid", 0), ("p_open", 0, 3),),
-     (("end", 1, 0), ("p_end", 1), ("end", 0, 1), ("p_mid", 0), ("end", 0, 3),)),
-    ("upg", 3, 4), ("down", 5, 6),
-    ("scatter",
-     (("end", 0, 0),),
-     (("p_open", 0, 3), ("end", 0, 0),)),
-    ("upg", 4, 6),
+     (("near", 0, 1), ("mid", 0, 1),),
+     (("near", 0, 3),)),
+    ("unpack", 1),
+    ("scatter",
+     (("p_open", 0, 2), ("end", 1, 0), ("p_end", 1),),
+     (("near", 0, 0), ("end", 0, 2), ("p_open", 0, 2),)),
+    ("upg", 0, 2),
+    ("scatter",
+     (),
+     (("p_end", 1),)),
+    ("upg", 2, 3),
+    ("scatter",
+     (("end", 0, 3), ("p_open", 0, 3), ("end", 0, 1), ("p_mid", 0), ("end", 0, 0),),
+     (("end", 0, 1), ("p_mid", 0), ("end", 0, 0), ("end", 0, 3), ("p_open", 0, 3),)),
+    ("down", 5, 6), ("upg", 3, 6),
     ("scatter",
      (("p_end", 0),),
      (("p_end", 0),)),
@@ -261,7 +264,6 @@
         loop(4, body)
 
     pack(grad_in, cg)
-    pack(tok_in, cx)
 
     barrier = pltpu.get_barrier_semaphore()
     partners = [dev_p(1), dev_p(3), dev_s(1), dev_s(3), dev(dy=2), sibling, far_z, zl1, zl2]
@@ -417,19 +419,21 @@
         loaded(1)
 
         def body(n):
-            cols = pl.ds(pl.multiple_of(n * 384, 128), 384)
+            cols = pl.ds(pl.multiple_of(n * 768, 256), 768)
             term = lax.dot_general(
                 hid[r * TOK:(r + 1) * TOK, :], wu[cols, :], NT, preferred_element_type=F32
             )
-            even, odd = r * 8 + 2 * n, r * 8 + 2 * n + 1
-            ci[even, 0:TOK, :] = term[:, 0:128].astype(BF)
-            ci[odd, 0:TOK, :] = term[:, 256:384].astype(BF)
-            top, bot = term[0:160, 128:256], swap_halves(term[160:320, 128:256])
             low = low_lanes((160, 128))
-            ci[even, TOK:BLK, :] = jnp.where(low, top, bot).astype(BF)
-            ci[odd, TOK:BLK, :] = jnp.where(low, bot, top).astype(BF)
-
-        loop(4, body)
+            for q in (0, 1):
+                even, lane = r * 8 + 4 * n + 2 * q, q * 384
+                ci[even, 0:TOK, :] = term[:, lane:lane + 128].astype(BF)
+                ci[even + 1, 0:TOK, :] = term[:, lane + 256:lane + 384].astype(BF)
+                mid = term[:, lane + 128:lane + 256]
+                top, bot = mid[0:160], swap_halves(mid[160:320])
+                ci[even, TOK:BLK, :] = jnp.where(low, top, bot).astype(BF)
+                ci[even + 1, TOK:BLK, :] = jnp.where(low, bot, top).astype(BF)
+
+        loop(2, body)
 
     def down(lo, hi):
         def body(i):
@@ -523,7 +527,11 @@
                 for name, *args in work:
                     scatter[name](*args)
 
+    packed = False
     for item in ORDER:
+        if item[0] == "tok" and not packed:
+            pack(tok_in, cx)
+            packed = True
         if item[0] == "scatter":
             by_core(0, item[1])
             by_core(1, item[2])

time: 116 us -> 107 us (0.922)
  Pallas kernels: 111 us -> 102 us
    pallas_call x1, Pallas kernels: 111 us -> 102 us  [per_device(): pl.pallas_call(kernel, out_shape=(jax.ShapeDtypeStruct((FEAT, TOK), BF),...]
where the time goes in v5:
time: 107 us; the launch traced here: 106 us
  Pallas kernels  102 us (95%)
  local copies, waits for them, and re-layouts  3.48 us (3%)
    pallas_call x1, Pallas kernels, per_device(): pl.pallas_call(kernel, out_shape=(jax.ShapeDtypeStruct((FEAT, TOK), BF),...  102 us
    unnamed x5, local copies, waits for them, and re-layouts  3.48 us

profile of v5, /device:TPU:32, one launch (start us, length us, event | category | flops | bytes accessed | tf_op | source)
XLA Modules:
  0.0 106.4 jit_solution(12233437029442164343)
XLA Ops:
  0.6 102.3 %ffn_backward.1 = (bf16[192,320]{1,0:T(8,128)(2,1)}, bf16[1536,768]{1,0:T(8,128)(2,1)S(1)}, bf16[768,1536]{1,0:T(8,128)(2,1)S(1)}) custom-call(bf16[192,320]{1,0:T(8,128)(2,1)} %bitcast.3, bf16[192,320]{1,0:T(8,128)(2,1)} %bitcast.4, bf16[320,3072]{1,0:T(8,128)(2,1)} %preact.1, bf16[1536,768]{1,0:T(8,128)(2,1)} %up_w.1, bf16[768,1536]{1,0:T(8,128)(2,1)} %down_w.1), custom_call_target="tpu_custom_call" | custom-call | tf_op jit(solution)/shard_map/ffn_backward/pallas_call | solution.py:568
  103.0 1.4 %copy.11 = bf16[1536,768]{1,0:T(8,128)(2,1)} copy(bf16[1536,768]{1,0:T(8,128)(2,1)S(1)} %get-tuple-element.10) | data formatting | bytes 4718592
  104.4 0.0 copy-start
  104.4 1.4 %copy.12 = bf16[768,1536]{1,0:T(8,128)(2,1)} copy(bf16[768,1536]{1,0:T(8,128)(2,1)S(1)} %get-tuple-element.11) | data formatting | bytes 4718592
  105.8 0.0 copy-done
  105.8 0.7 copy.13
Async XLA Ops:
  104.4 1.4 %copy-start = (bf16[192,320]{1,0:T(8,128)(2,1)S(1)}, bf16[192,320]{1,0:T(8,128)(2,1)}, u32[]{:S(2)}) copy-start(bf16[192,320]{1,0:T(8,128)(2,1)} %get-tuple-element.6) | copy-start | bytes 368644

commit v6 on v5

--- a/solution.py
+++ b/solution.py
@@ -18,119 +18,112 @@
 FWD = (0, 3)
 
 ORDER = (
-    ("grad", 0, 0, 0), ("grad",), ("grad", 0, 3, 0), ("grad", 0, 1, 0), ("grad", 1, 0, 0), ("tok",),
-    ("grad", 0, 0, 3), ("grad", 0, 2, 0), ("grad", 1, 0, 3), ("grad", 1, 1, 0), ("grad", 1, 3, 0),
-    ("grad", 0, 0, 2), ("grad", 0, 1, 1), ("activate", 0), ("grad", 0, 3, 1), ("grad", 0, 0, 1),
-    ("grad", 1, 0, 1), ("grad", 0, 3, 3), ("grad", 1, 0, 2), ("grad", 1, 2, 0), ("grad", 1, 1, 1), ("f1", 0),
-    ("grad", 1, 3, 3), ("grad", 0, 1, 2), ("grad", 0, 2, 1), ("grad", 1, 2, 1), ("pre_send",), ("grad", 1, 1, 3),
-    ("f2", 0), ("grad", 0, 1, 3), ("grad", 1, 1, 2), ("grad", 1, 3, 1), ("f1", 1), ("grad", 0, 2, 2),
-    ("grad", 0, 2, 3), ("grad", 0, 3, 2), ("tok", 1, 0, 0), ("grad", 1, 3, 2), ("grad", 1, 2, 3), ("f3", 0),
-    ("f2", 1), ("grad", 1, 2, 2), ("f1", 2), ("pre_relay",), ("f4", 0), ("tok", 0, 0, 0), ("f2", 2), ("f3", 1),
-    ("pre_get", 1), ("tok", 1, 1, 0), ("f5", 0), ("f1", 3), ("f3", 2), ("tok", 0, 3, 0), ("f4", 1),
-    ("tok", 0, 1, 0), ("pre_get", 2), ("tok", 0, 0, 1), ("tok", 0, 0, 3), ("f2", 3), ("activate", 1), ("f6", 0),
-    ("f4", 2), ("tok", 1, 2, 0), ("tok", 0, 2, 0), ("f5", 1), ("tok", 0, 3, 3), ("tok", 0, 1, 3),
-    ("tok", 1, 3, 0), ("tok", 0, 1, 1), ("f3", 3), ("f7", 0), ("tok", 1, 0, 3), ("f5", 2), ("f6", 1),
-    ("pre_get", 3), ("tok", 0, 2, 1), ("tok", 1, 2, 1),
+    ("grad",), ("grad", 0, 0, 0), ("tok", 0, 0, 0), ("grad", 0, 3, 0), ("grad", 0, 0, 1), ("grad", 0, 0, 3),
+    ("grad", 1, 0, 0), ("grad", 0, 1, 0), ("grad", 1, 1, 0), ("grad", 1, 0, 3), ("grad", 0, 1, 1),
+    ("grad", 1, 3, 0), ("tok",), ("grad", 0, 3, 3), ("grad", 0, 3, 1), ("grad", 1, 2, 0), ("grad", 0, 2, 0),
+    ("grad", 1, 1, 1), ("grad", 0, 0, 2), ("activate", 0), ("grad", 1, 0, 2), ("grad", 1, 1, 3),
+    ("grad", 1, 0, 1), ("f1", 0), ("grad", 0, 1, 3), ("grad", 1, 2, 1), ("grad", 1, 3, 3), ("grad", 0, 2, 1),
+    ("grad", 0, 3, 2), ("pre_send",), ("tok", 0, 1, 0), ("f2", 0), ("grad", 0, 1, 2), ("grad", 1, 3, 1),
+    ("grad", 1, 1, 2), ("f1", 1), ("grad", 1, 3, 2), ("grad", 1, 2, 2), ("grad", 0, 2, 3), ("grad", 1, 2, 3),
+    ("grad", 0, 2, 2), ("f1", 2), ("f2", 1), ("tok", 1, 0, 0), ("f2", 2), ("f3", 0), ("f1", 3), ("f3", 1),
+    ("pre_relay",), ("pre_get", 1), ("tok", 0, 0, 1), ("pre_get", 3), ("f3", 2), ("f2", 3), ("f4", 1),
+    ("tok", 0, 3, 0), ("tok", 1, 1, 0), ("pre_get", 2), ("f4", 2), ("tok", 1, 3, 0), ("f3", 3), ("activate", 2),
+    ("tok", 0, 3, 1), ("tok", 0, 2, 0), ("tok", 0, 1, 1), ("f5", 1), ("activate", 1), ("activate", 3),
+    ("down", 0, 1), ("f5", 2), ("tok", 1, 2, 0), ("down", 1, 2), ("tok", 0, 0, 3), ("tok", 1, 0, 3), ("f4", 3),
+    ("tok", 1, 0, 1), ("down", 2, 3), ("f6", 1), ("tok", 1, 3, 3), ("f4", 0), ("tok", 0, 3, 3), ("f6", 2),
+    ("tok", 1, 1, 1), ("tok", 0, 2, 3), ("tok", 0, 2, 1), ("down", 3, 4), ("tok", 1, 2, 1), ("f5", 3), ("f7", 1),
     ("scatter",
      (),
-     (("near", 1, 0), ("far", 0, 0),)),
-    ("f4", 3), ("tok", 0, 2, 3), ("tok", 1, 3, 3), ("f7", 1), ("f6", 2),
-    ("scatter",
-     (("near", 1, 2),),
-     (("far", 1, 0), ("far", 0, 1), ("far", 1, 1),)),
+     (("far", 1, 1),)),
+    ("f5", 0), ("f7", 2),
+    ("scatter",
+     (("near", 1, 2), ("far", 1, 1), ("far", 1, 3),),
+     ()),
+    ("f6", 3),
+    ("scatter",
+     (("far", 1, 2), ("far", 0, 3), ("near", 1, 1), ("far", 0, 2),),
+     (("near", 0, 1),)),
+    ("tok", 0, 1, 2),
+    ("scatter",
+     (),
+     (("near", 1, 2), ("far", 1, 2),)),
+    ("tok", 0, 2, 2),
+    ("scatter",
+     (("far", 0, 1),),
+     ()),
+    ("tok", 0, 1, 3),
+    ("scatter",
+     (),
+     (("near", 0, 2), ("mid", 1, 1), ("near", 1, 1),)),
+    ("tok", 0, 0, 2),
+    ("scatter",
+     (),
+     (("far", 0, 1), ("far", 0, 2),)),
+    ("tok", 1, 0, 2),
+    ("scatter",
+     (("far", 1, 0),),
+     ()),
+    ("f6", 0), ("tok", 0, 3, 2), ("f7", 3),
+    ("scatter",
+     (("mid", 1, 2), ("near", 1, 0), ("far", 0, 0),),
+     ()),
+    ("tok", 1, 1, 2),
+    ("scatter",
+     (),
+     (("far", 1, 3),)),
+    ("tok", 1, 3, 1),
+    ("scatter",
+     (("mid", 1, 1), ("near", 0, 2),),
+     (("mid", 1, 2),)),
+    ("tok", 1, 1, 3),
+    ("scatter",
+     (("near", 1, 3), ("mid", 0, 2), ("mid", 1, 3),),
+     (("near", 1, 3), ("far", 0, 3),)),
+    ("f7", 0),
+    ("scatter",
+     (("end", 1, 2), ("p_open", 1, 2),),
+     (("far", 1, 0), ("far", 0, 0),)),
+    ("unpack", 0), ("tok", 1, 2, 2), ("tok", 1, 3, 2),
+    ("scatter",
+     (("mid", 0, 3),),
+     ()),
     ("tok", 1, 2, 3),
     ("scatter",
-     (),
-     (("near", 0, 1),)),
-    ("f5", 3), ("tok", 1, 1, 1), ("tok", 0, 3, 2),
-    ("scatter",
-     (("near", 0, 2),),
-     ()),
-    ("tok", 1, 0, 2), ("activate", 3), ("f7", 2),
-    ("scatter",
-     (("far", 1, 3), ("far", 1, 1),),
-     (("mid", 1, 0),)),
-    ("f6", 3),
-    ("scatter",
-     (),
-     (("near", 1, 1),)),
-    ("activate", 2),
-    ("scatter",
-     (("far", 1, 2),),
-     ()),
-    ("tok", 0, 3, 1),
-    ("scatter",
-     (("far", 1, 0), ("far", 0, 0), ("far", 0, 1), ("far", 0, 3), ("near", 1, 1),),
-     (("far", 1, 2),)),
-    ("tok", 1, 3, 1), ("tok", 0, 0, 2),
-    ("scatter",
-     (("far", 0, 2),),
-     (("mid", 1, 1), ("mid", 0, 0),)),
-    ("tok", 1, 1, 2), ("f7", 3),
-    ("scatter",
-     (("mid", 1, 2),),
-     (("far", 1, 3), ("near", 1, 3), ("near", 1, 2), ("mid", 1, 2),)),
-    ("down", 0, 1),
-    ("scatter",
-     (("mid", 1, 1), ("near", 0, 3),),
-     (("far", 0, 3), ("end", 1, 0),)),
-    ("down", 1, 2),
-    ("scatter",
-     (("mid", 1, 3), ("mid", 0, 0),),
-     (("far", 0, 2), ("end", 1, 1),)),
-    ("tok", 1, 1, 3),
-    ("scatter",
-     (("near", 1, 3),),
-     ()),
-    ("down", 2, 3),
-    ("scatter",
-     (("end", 1, 2), ("p_open", 1, 2), ("mid", 0, 2),),
-     (("mid", 1, 3),)),
-    ("down", 3, 4),
-    ("scatter",
-     (),
-     (("end", 1, 2),)),
-    ("tok", 1, 3, 2),
-    ("scatter",
-     (("mid", 1, 0), ("end", 1, 1), ("p_open", 1, 1), ("near", 1, 0),),
-     (("p_open", 1, 2),)),
-    ("down", 4, 5), ("tok", 1, 0, 1),
-    ("scatter",
-     (("mid", 0, 3), ("end", 1, 3), ("p_mid", 1), ("near", 0, 0),),
-     (("near", 0, 2), ("mid", 0, 2),)),
-    ("unpack", 0),
-    ("scatter",
-     (),
-     (("p_open", 1, 1),)),
-    ("tok", 0, 1, 2),
-    ("scatter",
-     (),
-     (("mid", 0, 3),)),
+     (("near", 0, 1),),
+     ()),
     ("unpack", 3),
     ("scatter",
-     (),
-     (("end", 1, 3), ("mid", 0, 1), ("p_mid", 1),)),
-    ("tok", 1, 2, 2), ("tok", 0, 2, 2),
-    ("scatter",
-     (("end", 0, 2),),
-     ()),
+     (("mid", 1, 0), ("mid", 0, 0),),
+     (("mid", 0, 2), ("end", 1, 2), ("mid", 1, 3), ("p_open", 1, 2),)),
     ("unpack", 2),
     ("scatter",
-     (("near", 0, 1), ("mid", 0, 1),),
-     (("near", 0, 3),)),
+     (("end", 1, 1), ("p_open", 1, 1), ("near", 0, 3), ("end", 1, 3), ("p_mid", 1),),
+     (("mid", 0, 1), ("mid", 1, 0), ("near", 1, 0), ("end", 1, 1), ("near", 0, 0),)),
     ("unpack", 1),
     ("scatter",
-     (("p_open", 0, 2), ("end", 1, 0), ("p_end", 1),),
-     (("near", 0, 0), ("end", 0, 2), ("p_open", 0, 2),)),
-    ("upg", 0, 2),
+     (("end", 0, 2), ("mid", 0, 1), ("p_open", 0, 2),),
+     (("p_open", 1, 1), ("mid", 0, 0), ("near", 0, 3), ("end", 0, 2), ("end", 1, 3), ("p_mid", 1), ("mid", 0, 3), ("end", 0, 1), ("p_open", 0, 2),)),
+    ("down", 4, 5),
+    ("scatter",
+     (("near", 0, 0),),
+     ()),
+    ("upg", 0, 1),
+    ("scatter",
+     (("end", 0, 3), ("end", 1, 0), ("p_end", 1),),
+     (("end", 1, 0),)),
+    ("upg", 1, 2),
     ("scatter",
      (),
      (("p_end", 1),)),
     ("upg", 2, 3),
     ("scatter",
-     (("end", 0, 3), ("p_open", 0, 3), ("end", 0, 1), ("p_mid", 0), ("end", 0, 0),),
-     (("end", 0, 1), ("p_mid", 0), ("end", 0, 0), ("end", 0, 3), ("p_open", 0, 3),)),
-    ("down", 5, 6), ("upg", 3, 6),
+     (("end", 0, 1), ("p_mid", 0), ("p_open", 0, 3),),
+     (("p_mid", 0), ("end", 0, 3), ("end", 0, 0), ("p_open", 0, 3),)),
+    ("down", 5, 6), ("upg", 3, 4),
+    ("scatter",
+     (("end", 0, 0),),
+     ()),
+    ("upg", 4, 6),
     ("scatter",
      (("p_end", 0),),
      (("p_end", 0),)),
@@ -568,7 +561,7 @@
     input_grad, up_grad, down_grad = pl.pallas_call(
         kernel,
         out_shape=(
-            jax.ShapeDtypeStruct((FEAT, TOK), BF),
+            pltpu.VMEM((FEAT, TOK), BF),
             pltpu.VMEM((DI, HI), BF),
             pltpu.VMEM((HI, DI), BF),
         ),

time: 107 us -> 112 us (1.047)
  Pallas kernels: 102 us -> 108 us
    pallas_call x1, Pallas kernels: 102 us -> 108 us  [per_device(): pl.pallas_call(kernel, out_shape=(pltpu.VMEM((FEAT, TOK), BF), pltpu.VMEM...]
    unnamed x5 -> x3, local copies, waits for them, and re-layouts: 3.48 us -> 3.47 us
where the time goes in v6:
time: 112 us
  Pallas kernels  108 us (96%)
  local copies, waits for them, and re-layouts  3.47 us (3%)
    pallas_call x1, Pallas kernels, per_device(): pl.pallas_call(kernel, out_shape=(pltpu.VMEM((FEAT, TOK), BF), pltpu.VMEM...  108 us
    unnamed x3, local copies, waits for them, and re-layouts  3.47 us

profile of v6, /device:TPU:32, one launch (start us, length us, event | category | flops | bytes accessed | tf_op | source)
XLA Modules:
  0.0 112.0 jit_solution(17546111567941120502)
XLA Ops:
  0.6 107.9 %ffn_backward.1 = (bf16[192,320]{1,0:T(8,128)(2,1)S(1)}, bf16[1536,768]{1,0:T(8,128)(2,1)S(1)}, bf16[768,1536]{1,0:T(8,128)(2,1)S(1)}) custom-call(bf16[192,320]{1,0:T(8,128)(2,1)} %bitcast.4, bf16[192,320]{1,0:T(8,128)(2,1)} %bitcast.5, bf16[320,3072]{1,0:T(8,128)(2,1)} %preact.1, bf16[1536,768]{1,0:T(8,128)(2,1)} %up_w.1, bf16[768,1536]{1,0:T(8,128)(2,1)} %down_w.1), custom_call_target="tpu_custom_call" | custom-call | tf_op jit(solution)/shard_map/ffn_backward/pallas_call | solution.py:561
  108.5 0.7 copy.11
  109.2 1.4 %copy.12 = bf16[1536,768]{1,0:T(8,128)(2,1)} copy(bf16[1536,768]{1,0:T(8,128)(2,1)S(1)} %get-tuple-element.10) | data formatting | bytes 4718592
  110.6 1.4 %copy.13 = bf16[768,1536]{1,0:T(8,128)(2,1)} copy(bf16[768,1536]{1,0:T(8,128)(2,1)S(1)} %get-tuple-element.11) | data formatting | bytes 4718592

commit v7 on v5

--- a/solution.py
+++ b/solution.py
@@ -568,7 +568,7 @@
     input_grad, up_grad, down_grad = pl.pallas_call(
         kernel,
         out_shape=(
-            jax.ShapeDtypeStruct((FEAT, TOK), BF),
+            pltpu.VMEM((FEAT, TOK), BF),
             pltpu.VMEM((DI, HI), BF),
             pltpu.VMEM((HI, DI), BF),
         ),

time: 107 us -> 106 us (level)
    unnamed x5 -> x3, local copies, waits for them, and re-layouts: 3.48 us -> 3.47 us
where the time goes in v7:
time: 106 us
  Pallas kernels  101 us (95%)
  local copies, waits for them, and re-layouts  3.47 us (3%)
    pallas_call x1, Pallas kernels, per_device(): pl.pallas_call(kernel, out_shape=(pltpu.VMEM((FEAT, TOK), BF), pltpu.VMEM...  101 us
    unnamed x3, local copies, waits for them, and re-layouts  3.47 us

profile of v7, /device:TPU:32, one launch (start us, length us, event | category | flops | bytes accessed | tf_op | source)
XLA Modules:
  0.0 105.6 jit_solution(6838029619537770652)
XLA Ops:
  0.6 101.4 %ffn_backward.1 = (bf16[192,320]{1,0:T(8,128)(2,1)S(1)}, bf16[1536,768]{1,0:T(8,128)(2,1)S(1)}, bf16[768,1536]{1,0:T(8,128)(2,1)S(1)}) custom-call(bf16[192,320]{1,0:T(8,128)(2,1)} %bitcast.4, bf16[192,320]{1,0:T(8,128)(2,1)} %bitcast.5, bf16[320,3072]{1,0:T(8,128)(2,1)} %preact.1, bf16[1536,768]{1,0:T(8,128)(2,1)} %up_w.1, bf16[768,1536]{1,0:T(8,128)(2,1)} %down_w.1), custom_call_target="tpu_custom_call" | custom-call | tf_op jit(solution)/shard_map/ffn_backward/pallas_call | solution.py:568
  102.1 0.7 copy.11
  102.8 1.4 %copy.12 = bf16[1536,768]{1,0:T(8,128)(2,1)} copy(bf16[1536,768]{1,0:T(8,128)(2,1)S(1)} %get-tuple-element.10) | data formatting | bytes 4718592
  104.2 1.4 %copy.13 = bf16[768,1536]{1,0:T(8,128)(2,1)} copy(bf16[768,1536]{1,0:T(8,128)(2,1)S(1)} %get-tuple-element.11) | data formatting | bytes 4718592
